TPU v7x, 32 devices: a whole 2x2x4 slice. The times are simulated.
32 devices in a mesh: dp: 8 (over z, y), row: 4 (over x, core).
Axes of the slice: x: 2, y: 2, z: 4, core: 2. Of those that a mesh axis runs over, the one named last changes fastest.
Arguments:
- tokens: bfloat16 [24576, 768], P(('dp', 'row')), may hold values from -6 to 6
- ln_gain: float32 [768], replicated, may hold values from 0.5 to 1.5
- ln_bias: float32 [768], replicated, may hold values from -1.5 to 1.5
- w_query: bfloat16 [768, 768], P('dp', 'row'), may hold values from -0.21875 to 0.21875
- w_key: bfloat16 [768, 768], P('dp', 'row'), may hold values from -0.21875 to 0.21875
- w_value: bfloat16 [768, 768], P('dp', 'row'), may hold values from -0.21875 to 0.21875
- w_out: bfloat16 [768, 768], P('row', 'dp'), may hold values from -1.75 to 1.75
- w_up: bfloat16 [768, 3072], P('dp', 'row'), may hold values from -0.21875 to 0.21875
- w_down: bfloat16 [3072, 768], P('row', 'dp'), may hold values from -0.109375 to 0.109375
- doc_lengths: int32 [8, 4], P('dp'), may hold values from 1 to 1024, 3072 in all within a row
- cotangent: bfloat16 [24576, 768], P(('dp', 'row')), may hold values from -6 to 6
Outputs:
- mixed: bfloat16 [24576, 768], P(('dp', 'row'))
- input_grad: bfloat16 [24576, 768], P(('dp', 'row'))
- gain_grad: float32 [768], replicated
- bias_grad: float32 [768], replicated
- query_wgrad: float32 [768, 768], P('dp', 'row')
- key_wgrad: float32 [768, 768], P('dp', 'row')
- value_wgrad: float32 [768, 768], P('dp', 'row')
- out_wgrad: float32 [768, 768], P('row', 'dp')
- up_wgrad: float32 [768, 3072], P('dp', 'row')
- down_wgrad: float32 [3072, 768], P('row', 'dp')
Inputs may be any that keep to these rules, and one draw needn't show every extreme that they name: `doc_lengths`: row k lists the lengths of the 4 documents packed in order into the 3072 tokens of index k of dp; they sum to 3072 and the longest is exactly 1024.
All inputs are finite; a program needn't handle non-finite values.
Results may differ from a plain program's by a relative error of at most 0.0099.
Values may be sent and summed in bfloat16 or wider, within the bound.
No kernel may reach another device: no remote copies, remote signals or barrier semaphores. Data moves between devices by JAX's collectives and lax.ppermute only.
A program may use at most 128 MiB of HBM per device.

v0:
```python
from functools import partial
import math

import jax
import jax.numpy as jnp
from jax import lax
from jax.experimental import pallas as pl
from jax.experimental.pallas import tpu as pltpu
from jax.sharding import PartitionSpec as P

HEAD_DIM = 64
ROT_DIM = 16
HALF_ROT = ROT_DIM // 2
SEQ_MAX = 1024
QB = 256
EPS = 1e-05
MASKED = -1000000000.0
MIB = 1024 * 1024
F32 = jnp.float32
BF16 = jnp.bfloat16


def dot_nn(a, b):
    return lax.dot_general(a, b, (((1,), (0,)), ((), ())), preferred_element_type=F32)


def dot_nt(a, b):
    return lax.dot_general(a, b, (((1,), (1,)), ((), ())), preferred_element_type=F32)


def dot_tn(a, b):
    return lax.dot_general(a, b, (((0,), (0,)), ((), ())), preferred_element_type=F32)


def unit_of(rows):
    inputs = rows.astype(F32)
    average = jnp.mean(inputs, axis=1, keepdims=True)
    centered = inputs - average
    spread_sq = jnp.mean(centered * centered, axis=1, keepdims=True)
    inv_std = lax.rsqrt(spread_sq + EPS)
    return centered * inv_std, inv_std


def rope_t(field, cosine, sine):
    heads = field.shape[0] // HEAD_DIM
    pieces = []
    for h in range(heads):
        one = field[h * HEAD_DIM : (h + 1) * HEAD_DIM]
        first, second = one[:HALF_ROT], one[HALF_ROT:ROT_DIM]
        pieces += [
            first * cosine - second * sine,
            second * cosine + first * sine,
            one[ROT_DIM:],
        ]
    return jnp.concatenate(pieces, axis=0)


def params(limit=56):
    return pltpu.CompilerParams(vmem_limit_bytes=limit * MIB)


def placing(first, sub):
    def place(b, me_ref):
        return jnp.bitwise_xor(me_ref[0], first + b // sub) * sub + b % sub

    return place


def list_specs(block, width, sub, count):
    return [
        pl.BlockSpec((block, width), lambda b, m, k=k: (jnp.clip(b - k * sub, 0, sub - 1), 0))
        for k in range(count)
    ]


def waiting(kernel, scalars, operands, deps):
    ahead = scalars + operands

    def run(*refs):
        kernel(*refs[:ahead], *refs[ahead + deps :])

    return run


def of_list(refs):
    part = pl.num_programs(0) // len(refs)
    out = refs[0][...]
    for k in range(1, len(refs)):
        out = jnp.where(pl.program_id(0) >= k * part, refs[k][...], out)
    return out


def put_list(refs, value):
    part = pl.num_programs(0) // len(refs)
    for k, ref in enumerate(refs):

        @pl.when(pl.program_id(0) // part == k)
        def _():
            ref[...] = value


def cost(micros):
    return pl.CostEstimate(flops=int(micros * 9.612e+07), bytes_accessed=1, transcendentals=0)


def ffn_kernel(tok_a, tok_b, g_a, g_b, gain, bias, w_up, w_down_t, *rest):
    hid = w_up.shape[1]
    last = len(rest) > 5
    if last:
        sofar, normed, mlp_a, mlp_b, d_normed, weight_out, weight_g = rest
    else:
        normed, mlp_a, mlp_b, d_normed, weight_g = rest

    @pl.when(pl.program_id(0) == 0)
    def _():
        weight_g[...] = sofar[...] if last else jnp.zeros_like(weight_g)

    unit, _ = unit_of(of_list([tok_a, tok_b]))
    n, g = (unit * gain[...] + bias[...]).astype(BF16), of_list([g_a, g_b])
    normed[...] = n
    up_pre = dot_nn(n, w_up[...])
    d_hidden = dot_nn(g, w_down_t[...])
    cdf = 0.5 * (1.0 + lax.erf(up_pre * (2.0**-0.5)))
    pdf = jnp.exp(-0.5 * up_pre * up_pre) * ((2.0 * math.pi) ** -0.5)
    hidden = (up_pre * cdf).astype(BF16)
    d_up = (d_hidden * (cdf + up_pre * pdf)).astype(BF16)
    put_list([mlp_a, mlp_b], dot_nt(hidden, w_down_t[...]).astype(BF16))
    d_normed[...] = dot_nt(d_up, w_up[...]).astype(BF16)
    weight_g[:, :hid] += dot_tn(n, d_up)
    weight_g[:, hid:] += dot_tn(g, hidden)
    if last:

        @pl.when(pl.program_id(0) == pl.num_programs(0) - 1)
        def _():
            weight_out[...] = weight_g[...].astype(BF16)


def feed_forward(toks, grads, gain, bias, w_up, w_down_t, sofar, deps=(), block=384):
    shard, width = grads[0].shape
    count = 2 * shard
    hid = w_up.shape[1]
    sub = shard // block
    row = pl.BlockSpec((block, width), lambda b: (b, 0))
    half = [
        pl.BlockSpec((block, width), lambda b, k=k: (jnp.clip(b - k * sub, 0, sub - 1), 0))
        for k in range(2)
    ]
    one = pl.BlockSpec((1, width), lambda b: (0, 0))
    square = pl.BlockSpec((width, hid), lambda b: (0, 0))
    double = pl.BlockSpec((width, 2 * hid), lambda b: (0, 0))
    return pl.pallas_call(
        waiting(ffn_kernel, 0, 8 + len(sofar), len(deps)),
        grid=(2 * sub,),
        in_specs=half + half + [one, one, square, square] + [double] * len(sofar) + [pl.BlockSpec(memory_space=pl.ANY)] * len(deps),
        out_specs=[row] + half + [row, double],
        out_shape=[
            jax.ShapeDtypeStruct((count, width), BF16),
            jax.ShapeDtypeStruct((shard, width), BF16),
            jax.ShapeDtypeStruct((shard, width), BF16),
            jax.ShapeDtypeStruct((count, width), BF16),
            jax.ShapeDtypeStruct((width, 2 * hid), BF16 if sofar else F32),
        ],
        scratch_shapes=[pltpu.VMEM((width, 2 * hid), F32)] * len(sofar),
        compiler_params=params(),
        cost_estimate=cost(8),
        name="feed_forward",
    )(*toks, *grads, gain, bias, w_up, w_down_t, *sofar, *deps)


def assemble_kernel(me, part_a, part_b, part_c, part_d, out, last, whole):
    rows = part_a.shape[0]
    for k, part in enumerate((part_a, part_b, part_c, part_d)):
        whole[pl.ds(pl.multiple_of(jnp.bitwise_xor(me[0], k) * rows, rows), rows)] = part[...]
    turned = whole[...].T
    out[...] = turned
    last[...] = turned[3 * last.shape[0] :]


def assemble(me, parts):
    rows, width = parts[0].shape
    return pl.pallas_call(
        assemble_kernel,
        grid_spec=pltpu.PrefetchScalarGridSpec(
            num_scalar_prefetch=1,
            grid=(1,),
            in_specs=[pl.BlockSpec((rows, width), lambda b, m: (0, 0))] * 4,
            out_specs=[
                pl.BlockSpec((width, 4 * rows), lambda b, m: (0, 0)),
                pl.BlockSpec((width // 4, 4 * rows), lambda b, m: (0, 0)),
            ],
            scratch_shapes=[pltpu.VMEM((4 * rows, width), BF16)],
        ),
        out_shape=[
            jax.ShapeDtypeStruct((width, 4 * rows), BF16),
            jax.ShapeDtypeStruct((width // 4, 4 * rows), BF16),
        ],
        compiler_params=params(),
        cost_estimate=cost(3),
        name="assemble",
    )(me, *parts)


def project_kernel(me, n_a, n_b, g_a, g_b, g_c, g_d, wat, cosine, sine, qkv, d_ctx):
    low = of_list([n_a, n_b])
    width = d_ctx.shape[0]
    out = dot_nt(wat[: 3 * width], low)
    d_ctx[...] = dot_nt(wat[3 * width :], of_list([g_a, g_b, g_c, g_d])).astype(BF16)
    cos_b, sin_b = cosine[...], sine[...]
    scale = HEAD_DIM ** (-0.5)
    qkv[:width] = (rope_t(out[:width], cos_b, sin_b) * scale).astype(BF16)
    qkv[width : 2 * width] = rope_t(out[width : 2 * width], cos_b, sin_b).astype(BF16)
    qkv[2 * width :] = out[2 * width :].astype(BF16)


def project(me, normeds, grads, wat, cosine, sine, deps=(), block=384):
    shard, width = grads[0].shape
    total = cosine.shape[1]
    sub = shard // block
    own = width // 4
    place = placing(0, sub)
    table = pl.BlockSpec((HALF_ROT, block), lambda b, m: (0, place(b, m)))
    return pl.pallas_call(
        waiting(project_kernel, 1, 9, len(deps)),
        grid_spec=pltpu.PrefetchScalarGridSpec(
            num_scalar_prefetch=1,
            grid=(4 * sub,),
            in_specs=list_specs(block, width, 2 * sub, 2)
            + list_specs(block, width, sub, 4)
            + [pl.BlockSpec((4 * own, width), lambda b, m: (0, 0)), table, table]
            + [pl.BlockSpec(memory_space=pl.ANY)] * len(deps),
            out_specs=[
                pl.BlockSpec((3 * own, block), lambda b, m: (0, place(b, m))),
                pl.BlockSpec((own, block), lambda b, m: (0, place(b, m))),
            ],
        ),
        out_shape=[
            jax.ShapeDtypeStruct((3 * own, total), BF16),
            jax.ShapeDtypeStruct((own, total), BF16),
        ],
        compiler_params=params(),
        cost_estimate=cost(11),
        name="project",
    )(me, *normeds, *grads, wat, cosine, sine, *deps)


def attention_kernel(low_block, me, qkv, d_ctx, begin, cosine, sine, ctx_a, ctx_b, ctx_c, ctx_d, dq, kv, k_rows, v_rows, k_t, v_t, dk_t, dv_t):
    i = pl.program_id(0)
    width = d_ctx.shape[0]
    heads = width // HEAD_DIM
    here = pl.multiple_of(i * QB, QB)
    q_t = qkv[:width]
    k_here = qkv[width : 2 * width]
    v_here = qkv[2 * width :]
    k_t[:, pl.ds(here, QB)] = k_here
    v_t[:, pl.ds(here, QB)] = v_here
    k_nat = k_here.T
    v_nat = v_here.T
    for h in range(heads):
        cols = slice(h * HEAD_DIM, (h + 1) * HEAD_DIM)
        k_rows[h, pl.ds(here, QB), :] = k_nat[:, cols]
        v_rows[h, pl.ds(here, QB), :] = v_nat[:, cols]
    dk_t[:, pl.ds(here, QB)] = jnp.zeros((width, QB), F32)
    dv_t[:, pl.ds(here, QB)] = jnp.zeros((width, QB), F32)
    base = low_block[i]
    start = pl.multiple_of(base * QB, QB)
    reach = i - base
    first_key = begin[...] - start
    last_key = lax.broadcasted_iota(jnp.int32, (1, QB), 1) + (here - start)
    do_t = d_ctx[...]
    cos_here = cosine[:, pl.ds(here, QB)]
    sin_here = sine[:, pl.ds(here, QB)]
    scale = HEAD_DIM ** (-0.5)

    def run(blocks):
        span = blocks * QB
        key = lax.broadcasted_iota(jnp.int32, (span, QB), 0)
        allowed = (key >= first_key) & (key <= last_key)
        window = pl.ds(start, span)
        contexts = []
        for h in range(heads):
            rows = slice(h * HEAD_DIM, (h + 1) * HEAD_DIM)
            scores = dot_nn(k_rows[h, window, :], q_t[rows])
            scores = jnp.where(allowed, scores, MASKED)
            highest = jnp.max(scores, axis=0, keepdims=True)
            expo = jnp.exp(scores - highest)
            prob = expo * (1.0 / jnp.sum(expo, axis=0, keepdims=True))
            prob_low = prob.astype(BF16)
            context = dot_nn(v_t[rows, window], prob_low)
            d_prob = dot_nn(v_rows[h, window, :], do_t[rows])
            delta = jnp.sum(do_t[rows].astype(F32) * context, axis=0, keepdims=True)
            d_scores = (prob * (d_prob - delta)).astype(BF16)
            dq_h = dot_nn(k_t[rows, window], d_scores) * scale
            dq[rows] = rope_t(dq_h, cos_here, -sin_here).astype(BF16)
            contexts.append(context.astype(BF16))
            dk_t[rows, window] += dot_nt(q_t[rows], d_scores)
            dv_t[rows, window] += dot_nt(do_t[rows], prob_low)
        for j, ctx in enumerate((ctx_a, ctx_b, ctx_c, ctx_d)):

            @pl.when(i // (pl.num_programs(0) // 4) == jnp.bitwise_xor(me[0], j))
            def _():
                ctx[...] = jnp.concatenate(contexts, axis=0)

    for far in range(SEQ_MAX // QB + 1):
        pl.when(reach == far)(partial(run, far + 1))

    @pl.when(i == pl.num_programs(0) - 1)
    def _():
        kv[:width] = rope_t(dk_t[...], cosine[...], -sine[...]).astype(BF16)
        kv[width:] = dv_t[...].astype(BF16)


def attention(low_block, me, qkv, d_ctx, begin, cosine, sine, deps=()):
    width, total = d_ctx.shape
    heads = width // HEAD_DIM

    part = total // QB // 4

    def column(rows):
        return pl.BlockSpec((rows, QB), lambda i, m, r: (0, i))

    def whole(rows):
        return pl.BlockSpec((rows, total), lambda i, m, r: (0, 0))

    shards = [
        pl.BlockSpec(
            (width, QB),
            lambda i, m, r, j=j: (0, jnp.clip(i - jnp.bitwise_xor(r[0], j) * part, 0, part - 1)),
        )
        for j in range(4)
    ]

    return pl.pallas_call(
        waiting(attention_kernel, 2, 5, len(deps)),
        grid_spec=pltpu.PrefetchScalarGridSpec(
            num_scalar_prefetch=2,
            grid=(total // QB,),
            in_specs=[
                column(3 * width),
                column(width),
                column(1),
                whole(HALF_ROT),
                whole(HALF_ROT),
            ]
            + [pl.BlockSpec(memory_space=pl.ANY)] * len(deps),
            out_specs=shards + [column(width), whole(2 * width)],
            scratch_shapes=[
                pltpu.VMEM((heads, total, HEAD_DIM), BF16),
                pltpu.VMEM((heads, total, HEAD_DIM), BF16),
                pltpu.VMEM((width, total), BF16),
                pltpu.VMEM((width, total), BF16),
                pltpu.VMEM((width, total), F32),
                pltpu.VMEM((width, total), F32),
            ],
        ),
        out_shape=[jax.ShapeDtypeStruct((width, total // 4), BF16)] * 4
        + [
            jax.ShapeDtypeStruct((width, total), BF16),
            jax.ShapeDtypeStruct((2 * width, total), BF16),
        ],
        compiler_params=params(),
        cost_estimate=cost(46),
        name="attention",
    )(low_block, me, qkv, d_ctx, begin, cosine, sine, *deps)


def finish_kernel(last, me, *refs):
    ctx_a, ctx_b, dq, kv, tok_a, tok_b, g_a, g_b, normed, d_mlp, wat = refs[:11]
    if last:
        sums_in, total_in, dn_a, dn_b, sums, weight_g, total_g = refs[11:]
    else:
        dn_a, dn_b, sums, total_g = refs[11:]

    @pl.when(pl.program_id(0) == 0)
    def _():
        sums[...] = sums_in[...] if last else jnp.zeros_like(sums)
        total_g[...] = total_in[...] if last else jnp.zeros_like(total_g)

    own = dq.shape[0]
    n = normed[...]
    total = dot_nn(dq[...].T, wat[:own]) + dot_nn(kv[...].T, wat[own : 3 * own])
    total_g[:own] += dot_nn(dq[...], n)
    total_g[own : 3 * own] += dot_nn(kv[...], n)
    total_g[3 * own :] += dot_nn(of_list([ctx_a, ctx_b]), of_list([g_a, g_b]))
    total = total + d_mlp[...].astype(F32)
    unit, _ = unit_of(of_list([tok_a, tok_b]))
    sums[0:1] += jnp.sum(total * unit, axis=0, keepdims=True)
    sums[1:2] += jnp.sum(total, axis=0, keepdims=True)
    put_list([dn_a, dn_b], total.astype(BF16))
    if last:

        @pl.when(pl.program_id(0) == pl.num_programs(0) - 1)
        def _():
            weight_g[...] = total_g[...].T


def finish(me, ctxs, dq, kv, toks, grads, normed, d_mlp, wat, first, sofar=(), deps=(), block=384):
    shard, width = toks[0].shape
    sub = shard // block
    place = placing(first, sub)
    last = len(sofar) > 0

    def column(rows):
        return pl.BlockSpec((rows, block), lambda b, m: (0, place(b, m)))

    context = [
        pl.BlockSpec((width // 4, block), lambda b, m, k=k: (0, jnp.clip(b - k * sub, 0, sub - 1)))
        for k in range(2)
    ]
    two = list_specs(block, width, sub, 2)
    row = pl.BlockSpec((block, width), lambda b, m: (b, 0))
    square = pl.BlockSpec((width, width), lambda b, m: (0, 0))
    sums = pl.BlockSpec((8, width), lambda b, m: (0, 0))
    return pl.pallas_call(
        waiting(partial(finish_kernel, last), 1, 11 + len(sofar), len(deps)),
        grid_spec=pltpu.PrefetchScalarGridSpec(
            num_scalar_prefetch=1,
            grid=(2 * sub,),
            in_specs=context
            + [column(width // 4), column(width // 2)]
            + two
            + two
            + [row, row, square]
            + ([sums, square] if last else [])
            + [pl.BlockSpec(memory_space=pl.ANY)] * len(deps),
            out_specs=two + [sums, square],
            scratch_shapes=[pltpu.VMEM((width, width), F32)] if last else [],
        ),
        out_shape=[jax.ShapeDtypeStruct((shard, width), BF16)] * 2
        + [jax.ShapeDtypeStruct((8, width), F32), jax.ShapeDtypeStruct((width, width), F32)],
        compiler_params=params(),
        cost_estimate=cost(10),
        name="finish",
    )(me, *ctxs, dq, kv, *toks, *grads, normed, d_mlp, wat, *sofar, *deps)


def input_gradient_kernel(tok, cotangent, dn_a, dn_b, dn_c, gain, out):
    share = dn_a[...].astype(F32) + dn_b[...].astype(F32) + dn_c[...].astype(F32)
    unit, inv_std = unit_of(tok[...])
    unit_grad = share * gain[...]
    plain_mean = jnp.mean(unit_grad, axis=1, keepdims=True)
    cross_mean = jnp.mean(unit_grad * unit, axis=1, keepdims=True)
    out[...] = (
        cotangent[...].astype(F32) + inv_std * (unit_grad - plain_mean - unit * cross_mean)
    ).astype(BF16)


def input_gradient(tok, cotangent, dns, gain, deps=(), block=256):
    shard, width = tok.shape
    row = pl.BlockSpec((block, width), lambda b: (b, 0))
    return pl.pallas_call(
        waiting(input_gradient_kernel, 0, 6, len(deps)),
        grid=(shard // block,),
        in_specs=[row] * 5
        + [pl.BlockSpec((1, width), lambda b: (0, 0))]
        + [pl.BlockSpec(memory_space=pl.ANY)] * len(deps),
        out_specs=row,
        out_shape=jax.ShapeDtypeStruct((shard, width), BF16),
        compiler_params=params(),
        cost_estimate=cost(5),
        name="input_gradient",
    )(tok, cotangent, *dns, gain, *deps)


def mix_kernel(tok, mlp_a, mlp_b, mlp_c, *rest):
    ctxs, weights, mixed = rest[:4], rest[4:8], rest[8]
    total = tok[...].astype(F32) + mlp_a[...].astype(F32)
    total = total + (mlp_b[...].astype(F32) + mlp_c[...].astype(F32))
    for ctx, weight in zip(ctxs, weights):
        total = total + dot_nn(ctx[...].T, weight[...])
    mixed[...] = total.astype(BF16)


def mix(tok, mlps, ctxs, weights, deps=(), block=384):
    shard, width = tok.shape
    own = width // 4
    row = pl.BlockSpec((block, width), lambda b: (b, 0))
    return pl.pallas_call(
        waiting(mix_kernel, 0, 12, len(deps)),
        grid=(shard // block,),
        in_specs=[row] * 4
        + [pl.BlockSpec((own, block), lambda b: (0, b))] * 4
        + [pl.BlockSpec((own, width), lambda b: (0, 0))] * 4
        + [pl.BlockSpec(memory_space=pl.ANY)] * len(deps),
        out_specs=row,
        out_shape=jax.ShapeDtypeStruct((shard, width), BF16),
        compiler_params=params(),
        cost_estimate=cost(5),
        name="mix",
    )(tok, *mlps, *ctxs, *weights, *deps)


def together(*values, deps=()):
    def nothing(*refs):
        pass

    anywhere = pl.BlockSpec(memory_space=pl.ANY)
    return pl.pallas_call(
        nothing,
        in_specs=[anywhere] * (len(values) + len(deps)),
        out_specs=[anywhere] * len(values),
        out_shape=[jax.ShapeDtypeStruct(value.shape, value.dtype) for value in values],
        input_output_aliases={k: k for k in range(len(values))},
        cost_estimate=cost(1),
        name="together",
    )(*values, *deps)


def after(value, *deps):
    return together(value, deps=deps)[0]


def swap(value, axis, size, bit):
    return lax.ppermute(value, axis, [(i, i ^ bit) for i in range(size)])


def bits_of(size):
    out, bit = [], 1
    while bit < size:
        out.insert(0, bit)
        bit *= 2
    return out


class Gather:
    def __init__(self, shard, size, me):
        self.held, self.done, self.size, self.me = shard, [], size, me

    def send(self, bit):
        self.bit = bit
        self.theirs = swap(self.held, "dp", self.size, bit)

    def whole(self):
        return self.held.reshape(-1, self.held.shape[-1])


def merge_kernel(second, *refs):
    count = len(refs) // 3
    for k in range(count):
        held, theirs, out = refs[2 * k], refs[2 * k + 1], refs[2 * count + k]
        for high in range(held.shape[0]):
            out[high, second[k]] = held[high]
            out[high, 1 - second[k]] = theirs[high]


def merge(gathers, deps=()):
    second, parts, shapes = [], [], []
    for gather in gathers:
        second.append(((gather.me & gather.bit) != 0).astype(jnp.int32))
        high = 2 ** sum(1 for other in gather.done if other > gather.bit)
        gather.done.append(gather.bit)
        width = gather.held.shape[-1]
        one = (high, gather.held.size // (high * width), width)
        parts += [gather.held.reshape(one), gather.theirs.reshape(one)]
        shapes.append(jax.ShapeDtypeStruct((one[0], 2, *one[1:]), gather.held.dtype))

    def whole(shape):
        return pl.BlockSpec(shape, lambda b, m: (0,) * len(shape))

    outs = pl.pallas_call(
        waiting(merge_kernel, 1, len(parts), len(deps)),
        grid_spec=pltpu.PrefetchScalarGridSpec(
            num_scalar_prefetch=1,
            grid=(1,),
            in_specs=[whole(part.shape) for part in parts]
            + [pl.BlockSpec(memory_space=pl.ANY)] * len(deps),
            out_specs=[whole(shape.shape) for shape in shapes],
        ),
        out_shape=shapes,
        compiler_params=params(),
        cost_estimate=cost(2),
        name="merge",
    )(jnp.stack(second), *parts, *deps)
    for gather, out in zip(gathers, outs):
        gather.held = out


class Scatter:
    def __init__(self, whole, size, me):
        rows, width = whole.shape
        self.left, self.size, self.me = bits_of(size), size, me
        self.held = whole.reshape((2,) * len(self.left) + (rows // size, width))

    def send(self, bit, deps=()):
        axis = self.left.index(bit)
        self.left.remove(bit)
        mine = ((self.me & bit) != 0).astype(jnp.int32)
        self.keep = lax.dynamic_index_in_dim(self.held, mine, axis, keepdims=False)
        away = lax.dynamic_index_in_dim(self.held, 1 - mine, axis, keepdims=False)
        self.away = away.astype(BF16)
        if deps:
            self.away = after(self.away, *deps)
        self.theirs = swap(self.away, "dp", self.size, bit)

    def take(self):
        self.held = self.keep.astype(F32) + self.theirs.astype(F32)

    def send_last(self):
        high, low = self.left
        quarters = self.held.reshape(4, *self.held.shape[2:])
        place = (self.me // low) % 4
        self.keep = lax.dynamic_index_in_dim(quarters, place, 0, keepdims=False).astype(F32)
        self.aways = [
            lax.dynamic_index_in_dim(quarters, place ^ k, 0, keepdims=False).astype(BF16)
            for k in range(1, 4)
        ]
        self.parts = [swap(self.aways[k - 1], "dp", self.size, k * low) for k in range(1, 4)]

    def take_last(self):
        one, two, three = [part.astype(F32) for part in self.parts]
        self.held = (self.keep + one) + (two + three)


def sum_over(value, axis, size, bits):
    if len(bits) == 1:
        return value + swap(value, axis, size, bits[0])
    far, near = bits
    parts = together(*[swap(value, axis, size, bit) for bit in (near, far, far + near)])
    return (value + parts[0]) + (parts[1] + parts[2])


def tables(lengths, count):
    doc_ends = jnp.cumsum(lengths)
    places = jnp.arange(count, dtype=jnp.int32)
    after_end = places[:, None] >= doc_ends[None, :]
    begins = jnp.max(jnp.where(after_end, doc_ends[None, :], 0), axis=1)
    offset_f = (places - begins).astype(F32)
    frequency = jnp.exp(
        -(2.0 * jnp.arange(HALF_ROT, dtype=F32) / ROT_DIM) * math.log(10000.0)
    )
    angle = frequency[:, None] * offset_f[None, :]
    low_block = begins.reshape(count // QB, QB)[:, 0] // QB
    return begins[None, :], low_block, jnp.cos(angle), jnp.sin(angle)


def body(
    n_dp, n_row, tokens, ln_gain, ln_bias, w_query, w_key, w_value, w_out, w_up, w_down, doc_lengths, cotangent
):
    shard, width = tokens.shape
    total = shard * n_row
    own = width // n_row
    hid = w_up.shape[1]
    dp_me = lax.axis_index("dp")
    row_me = lax.axis_index("row").astype(jnp.int32)
    me = row_me.reshape(1)
    bits = bits_of(n_dp)
    to_core = partial(swap, axis="row", size=n_row, bit=1)
    to_chip = partial(swap, axis="row", size=n_row, bit=2)
    to_both = partial(swap, axis="row", size=n_row, bit=3)

    tok = [tokens, to_core(tokens), to_chip(tokens)]
    grad = [cotangent, to_core(cotangent)]
    up = Gather(w_up, n_dp, dp_me)
    down = Gather(w_down.T, n_dp, dp_me)
    orders = list(zip(bits, bits[-1:] + bits[:-1]))
    attn_shard = jnp.concatenate([w_query, w_key, w_value, w_out.T], axis=1)
    attn = Gather(attn_shard, n_dp, dp_me)
    for k, (first, second) in enumerate(orders):
        up.send(first)
        down.send(second)
        if k == 0:
            for bit in bits[:1:-1]:
                attn.send(bit)
                attn_ready = attn.theirs
                merge([attn])
        merge([up, down], (attn_ready, tok[2]) if k + 2 == len(orders) else ())
    grad.append(to_chip(cotangent))
    begin, low_block, cosine, sine = tables(doc_lengths[0], total)
    gain, bias = ln_gain[None, :], ln_bias[None, :]

    up_w, down_w = up.whole(), down.whole()
    quarter = attn.whole()
    quarters = [swap(quarter, "dp", n_dp, bit) for bit in (bits[1], bits[0], bits[0] + bits[1])]
    near_n, *near_mlp, near_dm, ffn_g = feed_forward(
        tok[:2], grad[:2], gain, bias, up_w, down_w, (), (quarter, cosine, sine, begin)
    )
    tok.append(to_core(after(tok[2], near_dm, *quarters)))
    grad[2] = after(grad[2], near_dm, *quarters)
    grad.append(to_core(grad[2]))
    wat, own_out = assemble((dp_me // bits[1]).astype(jnp.int32).reshape(1), [quarter, *quarters])
    far_n, *far_mlp, far_dm, ffn_g = feed_forward(
        tok[2:], grad[2:], gain, bias, up_w, down_w, (ffn_g,), (wat,)
    )
    ffn_wg = lax.psum_scatter(ffn_g, "dp", scatter_dimension=0, tiled=True)
    far_mlp_core = to_core(far_mlp[1])
    near_mlp_core = to_core(near_mlp[1])

    qkv, d_ctx = project(me, [near_n, far_n], grad, wat, cosine, sine)
    mlp_both = (far_mlp[0].astype(F32) + far_mlp_core.astype(F32)).astype(BF16)
    mlp_chip = to_chip(mlp_both)
    out_w = [own_out]
    out_w += [to_core(out_w[0]), to_chip(out_w[0]), to_both(out_w[0])]

    *ctx, dq, kv = attention(
        low_block, me, qkv, d_ctx, begin, cosine, sine, (mlp_both,)
    )

    ctxs = [ctx[0], to_core(ctx[1]), to_chip(ctx[2]), to_both(ctx[3])]
    far_dn, far_dn_b, *sofar = finish(
        me, ctx[2:], dq, kv, tok[2:], grad[2:], far_n, far_dm, wat, 2, (), (mlp_chip, *out_w[1:])
    )
    theirs = to_core(far_dn_b)
    both = (far_dn.astype(F32) + theirs.astype(F32)).astype(BF16)
    dn_chip = to_chip(both)
    near_dn, near_dn_b, sums, attn_g = finish(
        me, ctx[:2], dq, kv, tok[:2], grad[:2], near_n, near_dm, wat, 0, sofar,
        (both, ctxs[2], ctxs[3], ffn_wg),
    )
    dn_core = to_core(near_dn_b)
    attn_sum = Scatter(attn_g, n_dp, dp_me)
    for bit in bits[:2:-1]:
        attn_sum.send(bit)
        attn_sum.take()
        sums = sum_over(sums, "dp", n_dp, [bit])
    first = swap(sums, "dp", n_dp, bits[2])
    attn_sum.send(bits[2], (first,))
    sums = sum_over(sums + first, "dp", n_dp, bits[:2])
    sums = sum_over(sums, "row", n_row, [2, 1])
    mixed = mix(tokens, [near_mlp[0], near_mlp_core, mlp_chip], ctxs, out_w)
    attn_sum.theirs = after(attn_sum.theirs, sums, dn_chip, mixed)
    attn_sum.take()
    attn_sum.send_last()
    input_grad = input_gradient(
        tokens, cotangent, [near_dn, dn_core, dn_chip], gain, attn_sum.aways
    )
    attn_sum.parts[0] = after(attn_sum.parts[0], input_grad)
    attn_sum.take_last()

    attn_wg, ffn_wg = attn_sum.held, ffn_wg.astype(F32)
    return (
        mixed,
        input_grad,
        sums[0],
        sums[1],
        attn_wg[:, :own],
        attn_wg[:, own : 2 * own],
        attn_wg[:, 2 * own : 3 * own],
        attn_wg[:, 3 * own :].T,
        ffn_wg[:, :hid],
        ffn_wg[:, hid:].T,
    )


def solution(mesh):
    in_specs = (
        P(("dp", "row"), None),
        P(),
        P(),
        P("dp", "row"),
        P("dp", "row"),
        P("dp", "row"),
        P("row", "dp"),
        P("dp", "row"),
        P("row", "dp"),
        P("dp", None),
        P(("dp", "row"), None),
    )
    out_specs = (
        P(("dp", "row"), None),
        P(("dp", "row"), None),
        P(),
        P(),
        P("dp", "row"),
        P("dp", "row"),
        P("dp", "row"),
        P("row", "dp"),
        P("dp", "row"),
        P("row", "dp"),
    )
    sizes = (mesh.shape["dp"], mesh.shape["row"])
    return jax.shard_map(
        partial(body, *sizes), mesh=mesh, in_specs=in_specs, out_specs=out_specs, check_vma=False
    )
```

profile of v0, /device:TPU:0, one launch (start us, length us, event | category | flops | bytes accessed | tf_op | source)
XLA Modules:
  0.0 295.5 jit_solution(10073970940980659712)
XLA Ops:
  7.2 3.0 %collective-permute-start.7 = (bf16[768,768]{1,0:T(8,128)(2,1)}, bf16[768,768]{1,0:T(8,128)(2,1)S(1)}, u32[]{:S(2)}, u32[]{:S(2)}) collective-permute-start(bf16[768,768]{1,0:T(8,128)(2,1)} %refs_0_.5), channel_id=1, source_target_pairs={{0,2},{1,3},{2,0},{3,1},{4,6},{5,7},{6,4},{7,5},{8,10},{9,11},{10,... | collective-permute-start | bytes 3538952 | tf_op jit(solution)/shard_map/ppermute | solution.py:513
  10.2 1.5 collective-permute-start.3
  11.7 2.6 collective-permute-start.2
  14.9 1.8 collective-permute-done.3
  16.7 5.3 %collective-permute-done.2 = bf16[96,768]{1,0:T(8,128)(2,1)S(1)} collective-permute-done((bf16[96,768]{1,0:T(8,128)(2,1)}, bf16[96,768]{1,0:T(8,128)(2,1)S(1)}, u32[]{:S(2)}, u32[]{:S(2)}) %collective-permute-start.2) | collective-permute-done | bytes 147488 | tf_op jit(solution)/shard_map/ppermute | solution.py:513
  22.7 2.6 merge.4
  26.1 3.3 %collective-permute-start.5 = (bf16[1,2,96,768]{3,2,1,0:T(8,128)(2,1)}, bf16[1,2,96,768]{3,2,1,0:T(8,128)(2,1)S(1)}, u32[]{:S(2)}, u32[]{:S(2)}) collective-permute-start(bf16[1,2,96,768]{3,2,1,0:T(8,128)(2,1)} %get-tuple-element.51), channel_id=1, source_target_pairs={{0,16},{4,20},{8,24},{12,28},{16,0},{20,4},{24,8},{28,12},{1,17},{... | collective-permute-start | bytes 884744 | tf_op jit(solution)/shard_map/ppermute | solution.py:513
  32.4 4.1 %collective-permute-done.6.refs_5_ = bf16[96,768]{1,0:T(8,128)(2,1)S(1)} collective-permute-done((bf16[96,768]{1,0:T(8,128)(2,1)S(1)}, bf16[96,768]{1,0:T(8,128)(2,1)S(1)}, u32[]{:S(2)}, u32[]{:S(2)}) %collective-permute-start.6) | collective-permute-done | bytes 147488 | tf_op jit(solution)/shard_map/ppermute | solution.py:513
  36.5 3.4 %collective-permute-done.4 = bf16[1,2,96,768]{3,2,1,0:T(8,128)(2,1)S(1)} collective-permute-done((bf16[1,2,96,768]{3,2,1,0:T(8,128)(2,1)}, bf16[1,2,96,768]{3,2,1,0:T(8,128)(2,1)S(1)}, u32[]{:S(2)}, u32[]{:S(2)}) %collective-permute-start.4) | collective-permute-done | bytes 294944 | tf_op jit(solution)/shard_map/ppermute | solution.py:513
  39.9 2.9 collective-permute-done.5
  44.0 3.1 %merge.5 = (bf16[2,2,96,768]{3,2,1,0:T(8,128)(2,1)}, bf16[1,2,192,768]{3,2,1,0:T(8,128)(2,1)}) custom-call(s32[2]{0:T(128)} %pad_add_fusion.1.refs_0_, bf16[2,96,768]{2,1,0:T(8,128)(2,1)} %bitcast.70, bf16[2,96,768]{2,1,0:T(8,128)(2,1)} %bitcast.72, bf16[1,192,768]{2,1,0:T(8,128)(2,1)} %bitcast.71, bf16[1,192,768]{2,1,0:T(8,128)(2,1)} %bitcast.73, ...), custom_call_target="tpu_custom_call" | custom-call | flops 192240000 | bytes 1 | tf_op jit(solution)/shard_map/merge/pallas_call | solution.py:559
  49.2 1.6 fusion.5.refs_1_
  51.6 1.7 merge.7
  53.4 2.0 collective-permute-start.13
  55.4 2.9 collective-permute-done.8
  58.3 3.2 %collective-permute-start.12 = (bf16[192,768]{1,0:T(8,128)(2,1)}, bf16[192,768]{1,0:T(8,128)(2,1)}, u32[]{:S(2)}, u32[]{:S(2)}) collective-permute-start(bf16[192,768]{1,0:T(8,128)(2,1)} %bitcast.62), channel_id=1, source_target_pairs={{0,16},{4,20},{8,24},{12,28},{16,0},{20,4},{24,8},{28,12},{1,17},{... | collective-permute-start | bytes 884744 | tf_op jit(solution)/shard_map/ppermute | solution.py:513
  62.1 2.7 collective-permute-start.11
  66.5 1.3 broadcast_in_dim.15.refs_5_
  69.4 3.8 %merge.6 = (bf16[4,2,96,768]{3,2,1,0:T(8,128)(2,1)}, bf16[2,2,192,768]{3,2,1,0:T(8,128)(2,1)}) custom-call(s32[2]{0:T(128)} %pad_add_fusion.refs_0_, bf16[4,96,768]{2,1,0:T(8,128)(2,1)} %bitcast.66, bf16[4,96,768]{2,1,0:T(8,128)(2,1)} %bitcast.14.refs_2_, bf16[2,192,768]{2,1,0:T(8,128)(2,1)} %bitcast.67, bf16[2,192,768]{2,1,0:T(8,128)(2,1)} %bitcast.16.refs_4_), custom_call_target="tpu_custom_call" | custom-call | flops 192240000 | bytes 1 | tf_op jit(solution)/shard_map/merge/pallas_call | solution.py:559
  73.2 21.7 %feed_forward.2 = (bf16[1536,768]{1,0:T(8,128)(2,1)}, bf16[768,768]{1,0:T(8,128)(2,1)}, bf16[768,768]{1,0:T(8,128)(2,1)}, bf16[1536,768]{1,0:T(8,128)(2,1)}, f32[768,1536]{1,0:T(8,128)}) custom-call(bf16[768,768]{1,0:T(8,128)(2,1)} %refs_0_.5, bf16[768,768]{1,0:T(8,128)(2,1)} %collective-permute-done.refs_1_.refs_6_, bf16[768,768]{1,0:T(8,128)(2,1)} %refs_1_.1, ...), custom_call_target="tpu_custom_call" | custom-call | flops 768960000 | bytes 1 | tf_op jit(solution)/shard_map/feed_forward/pallas_call | solution.py:151
  96.5 2.8 assemble.1
  100.7 23.2 %feed_forward.3 = (bf16[1536,768]{1,0:T(8,128)(2,1)}, bf16[768,768]{1,0:T(8,128)(2,1)}, bf16[768,768]{1,0:T(8,128)(2,1)}, bf16[1536,768]{1,0:T(8,128)(2,1)}, bf16[768,1536]{1,0:T(8,128)(2,1)}) custom-call(bf16[768,768]{1,0:T(8,128)(2,1)} %copy-done, bf16[768,768]{1,0:T(8,128)(2,1)} %collective-permute-done.14.refs_1_.refs_6_, ...), custom_call_target="tpu_custom_call" | custom-call | flops 768960000 | bytes 1 | tf_op jit(solution)/shard_map/feed_forward/pallas_call | solution.py:151
  124.0 1.2 copy-done.39
  125.3 2.7 collective-permute-done.17
  131.5 11.5 %project.1 = (bf16[576,3072]{1,0:T(8,128)(2,1)}, bf16[192,3072]{1,0:T(8,128)(2,1)}) custom-call(s32[1]{0:T(128)} %bitcast.26.refs_0_.refs_1_, bf16[1536,768]{1,0:T(8,128)(2,1)} %get-tuple-element.63.refs_1_.refs_9_, bf16[1536,768]{1,0:T(8,128)(2,1)} %get-tuple-element.64.refs_2_.refs_9_, bf16[768,768]{1,0:T(8,128)(2,1)} %refs_1_.1, ...), custom_call_target="tpu_custom_call" | custom-call | flops 1057320000 | bytes 1 | tf_op jit(solution)/shard_map/project/pallas_call | solution.py:222
  143.1 47.3 %attention.1 = (bf16[192,768]{1,0:T(8,128)(2,1)}, bf16[192,768]{1,0:T(8,128)(2,1)}, bf16[192,768]{1,0:T(8,128)(2,1)}, bf16[192,768]{1,0:T(8,128)(2,1)}, bf16[192...) custom-call(s32[12]{0:T(128)} %and_select_fusion.refs_0_, s32[1]{0:T(128)} %bitcast.26.refs_0_.refs_1_, ...), custom_call_target="tpu_custom_call" | custom-call | flops 4421519872 | bytes 1 | tf_op jit(solution)/shard_map/attention/pallas_call | solution.py:332
  191.6 11.0 %finish.2 = (bf16[768,768]{1,0:T(8,128)(2,1)}, bf16[768,768]{1,0:T(8,128)(2,1)}, f32[8,768]{1,0:T(8,128)}, f32[768,768]{1,0:T(8,128)}) custom-call(s32[1]{0:T(128)} %bitcast.26.refs_0_.refs_1_, bf16[192,768]{1,0:T(8,128)(2,1)} %get-tuple-element.69.refs_1_, bf16[192,768]{1,0:T(8,128)(2,1)} %get-tuple-element.70.refs_2_, ...), custom_call_target="tpu_custom_call" | custom-call | flops 961200000 | bytes 1 | tf_op jit(solution)/shard_map/finish/pallas_call | solution.py:413
  203.2 1.5 collective-permute-start.20
  205.8 1.6 add_convert_fusion.refs_14_
  207.4 2.4 collective-permute-start.27
  209.8 3.3 %collective-permute-done.20.refs_6_.refs_15_ = bf16[192,768]{1,0:T(8,128)(2,1)S(1)} collective-permute-done((bf16[192,768]{1,0:T(8,128)(2,1)S(1)}, bf16[192,768]{1,0:T(8,128)(2,1)S(1)}, u32[]{:S(2)}, u32[]{:S(2)}) %collective-permute-start.20) | collective-permute-done | bytes 294944 | tf_op jit(solution)/shard_map/ppermute | solution.py:513
  213.1 5.3 %collective-permute-done.21.refs_7_.refs_16_ = bf16[192,768]{1,0:T(8,128)(2,1)S(1)} collective-permute-done((bf16[192,768]{1,0:T(8,128)(2,1)S(1)}, bf16[192,768]{1,0:T(8,128)(2,1)S(1)}, u32[]{:S(2)}, u32[]{:S(2)}) %collective-permute-start.21) | collective-permute-done | bytes 294944 | tf_op jit(solution)/shard_map/ppermute | solution.py:513
  219.1 12.4 %finish.3 = (bf16[768,768]{1,0:T(8,128)(2,1)}, bf16[768,768]{1,0:T(8,128)(2,1)}, f32[8,768]{1,0:T(8,128)}, f32[768,768]{1,0:T(8,128)}) custom-call(s32[1]{0:T(128)} %bitcast.26.refs_0_.refs_1_, bf16[192,768]{1,0:T(8,128)(2,1)} %get-tuple-element.67.refs_4_.refs_1_, bf16[192,768]{1,0:T(8,128)(2,1)} %get-tuple-element.68.refs_2_, ...), custom_call_target="tpu_custom_call" | custom-call | flops 961200000 | bytes 1 | tf_op jit(solution)/shard_map/finish/pallas_call | solution.py:413
  232.2 3.6 %collective-permute-done.28.refs_1_ = f32[8,768]{1,0:T(8,128)S(1)} collective-permute-done((f32[8,768]{1,0:T(8,128)}, f32[8,768]{1,0:T(8,128)S(1)}, u32[]{:S(2)}, u32[]{:S(2)}) %collective-permute-start.28) | collective-permute-done | bytes 24608 | tf_op jit(solution)/shard_map/ppermute | solution.py:513
  236.5 5.2 %collective-permute-start.32 = (f32[8,768]{1,0:T(8,128)S(1)}, f32[8,768]{1,0:T(8,128)S(1)}, u32[]{:S(2)}, u32[]{:S(2)}) collective-permute-start(f32[8,768]{1,0:T(8,128)S(1)} %add.72), channel_id=1, source_target_pairs={{0,24},{4,28},{8,16},{12,20},{16,8},{20,12},{24,0},{28,4},{1,25},{... | collective-permute-start | bytes 73736 | tf_op jit(solution)/shard_map/ppermute | solution.py:513
  241.8 4.2 %collective-permute-start.31 = (f32[8,768]{1,0:T(8,128)S(1)}, f32[8,768]{1,0:T(8,128)S(1)}, u32[]{:S(2)}, u32[]{:S(2)}) collective-permute-start(f32[8,768]{1,0:T(8,128)S(1)} %add.72), channel_id=1, source_target_pairs={{0,16},{4,20},{8,24},{12,28},{16,0},{20,4},{24,8},{28,12},{1,17},{... | collective-permute-start | bytes 73736 | tf_op jit(solution)/shard_map/ppermute | solution.py:513
  246.0 2.2 collective-permute-start.30
  248.2 2.1 fusion.refs_0_
  250.5 2.0 collective-permute-start.29
  254.8 5.1 %mix.1.refs_3_ = bf16[768,768]{1,0:T(8,128)(2,1)} custom-call(bf16[768,768]{1,0:T(8,128)(2,1)} %refs_0_.5, bf16[768,768]{1,0:T(8,128)(2,1)} %get-tuple-element.56.refs_1_, bf16[768,768]{1,0:T(8,128)(2,1)} %collective-permute-done.10.refs_2_, bf16[768,768]{1,0:T(8,128)(2,1)} %copy-done.6, bf16[192,768]{1,0:T(8,128)(2,1)} %get-tuple-element.67.refs_4_.refs_1_, ...), custom_call_target="tpu_custom_call" | custom-call | flops 480600000 | bytes 1 | tf_op jit(solution)/shard_map/mix/pallas_call | solution.py:477
  262.7 1.2 collective-permute-done.34.refs_1_
  265.1 1.4 add_add_fusion.refs_1_
  268.4 1.6 bitcast_add_fusion
  270.0 2.9 collective-permute-start.38
  272.9 1.6 collective-permute-start.36
  274.5 1.4 slice_reduce_fusion.1
  275.9 5.7 %input_gradient.1.refs_1_ = bf16[768,768]{1,0:T(8,128)(2,1)} custom-call(bf16[768,768]{1,0:T(8,128)(2,1)} %refs_0_.5, bf16[768,768]{1,0:T(8,128)(2,1)} %refs_1_.1, bf16[768,768]{1,0:T(8,128)(2,1)} %get-tuple-element.80.refs_2_, bf16[768,768]{1,0:T(8,128)(2,1)} %collective-permute-done.26.refs_3_, bf16[768,768]{1,0:T(8,128)(2,1)} %copy-done.7, ...), custom_call_target="tpu_custom_call" | custom-call | flops 480600000 | bytes 1 | tf_op jit(solution)/shard_map/input_gradient/pallas_call | solution.py:450
  282.7 3.4 %collective-permute-done.37 = bf16[96,768]{1,0:T(8,128)(2,1)S(1)} collective-permute-done((bf16[96,768]{1,0:T(8,128)(2,1)S(1)}, bf16[96,768]{1,0:T(8,128)(2,1)S(1)}, u32[]{:S(2)}, u32[]{:S(2)}) %collective-permute-start.37) | collective-permute-done | bytes 147488 | tf_op jit(solution)/shard_map/ppermute | solution.py:513
  (171 shorter events, 36.3 us)
Async XLA Ops:
  7.2 211.2 %reduce-scatter.2.cloned.1.call-start = ((), (), s32[]{:S(2)}) async-start(), calls=%async_computation.1 | async-start | bytes 2654208 | tf_op jit(solution)/shard_map/reduce_scatter | solution.py:683
  7.2 35.6 %collective-permute-start.7 = (bf16[768,768]{1,0:T(8,128)(2,1)}, bf16[768,768]{1,0:T(8,128)(2,1)S(1)}, u32[]{:S(2)}, u32[]{:S(2)}) collective-permute-start(bf16[768,768]{1,0:T(8,128)(2,1)} %refs_0_.5), channel_id=1, source_target_pairs={{0,2},{1,3},{2,0},{3,1},{4,6},{5,7},{6,4},{7,5},{8,10},{9,11},{10,... | collective-permute-start | bytes 3538952 | tf_op jit(solution)/shard_map/ppermute | solution.py:513
  10.2 43.1 %collective-permute-start = (bf16[768,768]{1,0:T(8,128)(2,1)}, bf16[768,768]{1,0:T(8,128)(2,1)}, u32[]{:S(2)}, u32[]{:S(2)}) collective-permute-start(bf16[768,768]{1,0:T(8,128)(2,1)} %refs_0_.5), channel_id=1, source_target_pairs={{0,1},{1,0},{2,3},{3,2},{4,5},{5,4},{6,7},{7,6},{8,9},{9,8},{10,11... | collective-permute-start | bytes 3538952 | tf_op jit(solution)/shard_map/ppermute | solution.py:513
  10.2 6.5 %collective-permute-start.3 = (bf16[96,768]{1,0:T(8,128)(2,1)}, bf16[96,768]{1,0:T(8,128)(2,1)S(1)}, u32[]{:S(2)}, u32[]{:S(2)}) collective-permute-start(bf16[96,768]{1,0:T(8,128)(2,1)} %bitcast.79), channel_id=1, source_target_pairs={{0,4},{4,0},{8,12},{12,8},{16,20},{20,16},{24,28},{28,24},{1,5},{5... | collective-permute-start | bytes 442376 | tf_op jit(solution)/shard_map/ppermute | solution.py:513
  11.7 10.2 %collective-permute-start.2 = (bf16[96,768]{1,0:T(8,128)(2,1)}, bf16[96,768]{1,0:T(8,128)(2,1)S(1)}, u32[]{:S(2)}, u32[]{:S(2)}) collective-permute-start(bf16[96,768]{1,0:T(8,128)(2,1)} %param.18), channel_id=1, source_target_pairs={{0,16},{4,20},{8,24},{12,28},{16,0},{20,4},{24,8},{28,12},{1,17},{... | collective-permute-start | bytes 442376 | tf_op jit(solution)/shard_map/ppermute | solution.py:513
  25.3 14.6 %collective-permute-start.4 = (bf16[1,2,96,768]{3,2,1,0:T(8,128)(2,1)}, bf16[1,2,96,768]{3,2,1,0:T(8,128)(2,1)S(1)}, u32[]{:S(2)}, u32[]{:S(2)}) collective-permute-start(bf16[1,2,96,768]{3,2,1,0:T(8,128)(2,1)} %get-tuple-element.50), channel_id=1, source_target_pairs={{0,8},{4,12},{8,0},{12,4},{16,24},{20,28},{24,16},{28,20},{1,9},{5... | collective-permute-start | bytes 884744 | tf_op jit(solution)/shard_map/ppermute | solution.py:513
  26.1 16.8 %collective-permute-start.5 = (bf16[1,2,96,768]{3,2,1,0:T(8,128)(2,1)}, bf16[1,2,96,768]{3,2,1,0:T(8,128)(2,1)S(1)}, u32[]{:S(2)}, u32[]{:S(2)}) collective-permute-start(bf16[1,2,96,768]{3,2,1,0:T(8,128)(2,1)} %get-tuple-element.51), channel_id=1, source_target_pairs={{0,16},{4,20},{8,24},{12,28},{16,0},{20,4},{24,8},{28,12},{1,17},{... | collective-permute-start | bytes 884744 | tf_op jit(solution)/shard_map/ppermute | solution.py:513
  30.2 12.6 %copy-start.21 = (bf16[192,96]{0,1:T(8,128)(2,1)}, bf16[192,96]{0,1:T(8,128)(2,1)S(1)}, u32[]{:S(2)}) copy-start(bf16[192,96]{0,1:T(8,128)(2,1)S(1)} %copy.40) | copy-start | bytes 110596
  31.2 5.3 %collective-permute-start.6 = (bf16[96,768]{1,0:T(8,128)(2,1)S(1)}, bf16[96,768]{1,0:T(8,128)(2,1)S(1)}, u32[]{:S(2)}, u32[]{:S(2)}) collective-permute-start(bf16[96,768]{1,0:T(8,128)(2,1)S(1)} %pad_maximum_fusion), channel_id=1, source_target_pairs={{0,4},{4,0},{8,12},{12,8},{16,20},{20,16},{24,28},{28,24},{1,5},{5... | collective-permute-start | bytes 442376 | tf_op jit(solution)/shard_map/ppermute | solution.py:513
  47.1 18.8 %copy-start.38 = (f32[768]{0:T(1024)S(1)}, f32[768]{0:T(1024)}, u32[]{:S(2)}) copy-start(f32[768]{0:T(1024)} %param.12) | copy-start | bytes 9220
  47.1 21.2 %copy-start.1 = (bf16[768,768]{1,0:T(8,128)(2,1)S(1)}, bf16[768,768]{1,0:T(8,128)(2,1)}, u32[]{:S(2)}) copy-start(bf16[768,768]{1,0:T(8,128)(2,1)} %copy-done) | copy-start | bytes 3538948
  47.1 11.2 %collective-permute-start.8 = (bf16[2,2,96,768]{3,2,1,0:T(8,128)(2,1)}, bf16[2,2,96,768]{3,2,1,0:T(8,128)(2,1)}, u32[]{:S(2)}, u32[]{:S(2)}) collective-permute-start(bf16[2,2,96,768]{3,2,1,0:T(8,128)(2,1)} %get-tuple-element.52), channel_id=1, source_target_pairs={{0,4},{4,0},{8,12},{12,8},{16,20},{20,16},{24,28},{28,24},{1,5},{5... | collective-permute-start | bytes 1769480 | tf_op jit(solution)/shard_map/ppermute | solution.py:513
  47.6 14.4 %collective-permute-start.9 = (bf16[1,2,192,768]{3,2,1,0:T(8,128)(2,1)}, bf16[1,2,192,768]{3,2,1,0:T(8,128)(2,1)}, u32[]{:S(2)}, u32[]{:S(2)}) collective-permute-start(bf16[1,2,192,768]{3,2,1,0:T(8,128)(2,1)} %get-tuple-element.53), channel_id=1, source_target_pairs={{0,8},{4,12},{8,0},{12,4},{16,24},{20,28},{24,16},{28,20},{1,9},{5... | collective-permute-start | bytes 1769480 | tf_op jit(solution)/shard_map/ppermute | solution.py:513
  48.0 47.0 %collective-permute-start.15 = (bf16[768,768]{1,0:T(8,128)(2,1)S(1)}, bf16[768,768]{1,0:T(8,128)(2,1)S(1)}, u32[]{:S(2)}, u32[]{:S(2)}) collective-permute-start(bf16[768,768]{1,0:T(8,128)(2,1)S(1)} %copy-done.3), channel_id=1, source_target_pairs={{0,2},{1,3},{2,0},{3,1},{4,6},{5,7},{6,4},{7,5},{8,10},{9,11},{10,... | collective-permute-start | bytes 3538952 | tf_op jit(solution)/shard_map/ppermute | solution.py:513
  48.5 24.7 %collective-permute-start.1 = (bf16[768,768]{1,0:T(8,128)(2,1)S(1)}, bf16[768,768]{1,0:T(8,128)(2,1)}, u32[]{:S(2)}, u32[]{:S(2)}) collective-permute-start(bf16[768,768]{1,0:T(8,128)(2,1)S(1)} %copy-done.3), channel_id=1, source_target_pairs={{0,1},{1,0},{2,3},{3,2},{4,5},{5,4},{6,7},{7,6},{8,9},{9,8},{10,11... | collective-permute-start | bytes 3538952 | tf_op jit(solution)/shard_map/ppermute | solution.py:513
  51.6 17.8 %copy-start.28 = (s32[3072]{0:T(1024)}, s32[3072]{0:T(1024)S(1)}, u32[]{:S(2)}) copy-start(s32[3072]{0:T(1024)S(1)} %select_reduce_fusion) | copy-start | bytes 36868
  53.4 41.5 %collective-permute-start.13 = (bf16[192,768]{1,0:T(8,128)(2,1)}, bf16[192,768]{1,0:T(8,128)(2,1)}, u32[]{:S(2)}, u32[]{:S(2)}) collective-permute-start(bf16[192,768]{1,0:T(8,128)(2,1)} %bitcast.61), channel_id=1, source_target_pairs={{0,24},{4,28},{8,16},{12,20},{16,8},{20,12},{24,0},{28,4},{1,25},{... | collective-permute-start | bytes 884744 | tf_op jit(solution)/shard_map/ppermute | solution.py:513
  58.3 36.5 %collective-permute-start.12 = (bf16[192,768]{1,0:T(8,128)(2,1)}, bf16[192,768]{1,0:T(8,128)(2,1)}, u32[]{:S(2)}, u32[]{:S(2)}) collective-permute-start(bf16[192,768]{1,0:T(8,128)(2,1)} %bitcast.62), channel_id=1, source_target_pairs={{0,16},{4,20},{8,24},{12,28},{16,0},{20,4},{24,8},{28,12},{1,17},{... | collective-permute-start | bytes 884744 | tf_op jit(solution)/shard_map/ppermute | solution.py:513
  62.1 32.8 %collective-permute-start.11 = (bf16[192,768]{1,0:T(8,128)(2,1)}, bf16[192,768]{1,0:T(8,128)(2,1)}, u32[]{:S(2)}, u32[]{:S(2)}) collective-permute-start(bf16[192,768]{1,0:T(8,128)(2,1)} %bitcast.63), channel_id=1, source_target_pairs={{0,8},{4,12},{8,0},{12,4},{16,24},{20,28},{24,16},{28,20},{1,9},{5... | collective-permute-start | bytes 884744 | tf_op jit(solution)/shard_map/ppermute | solution.py:513
  94.9 4.4 %collective-permute-start.14 = (bf16[768,768]{1,0:T(8,128)(2,1)}, bf16[768,768]{1,0:T(8,128)(2,1)}, u32[]{:S(2)}, u32[]{:S(2)}) collective-permute-start(bf16[768,768]{1,0:T(8,128)(2,1)} %together.7), channel_id=1, source_target_pairs={{0,1},{1,0},{2,3},{3,2},{4,5},{5,4},{6,7},{7,6},{8,9},{9,8},{10,11... | collective-permute-start | bytes 3538952 | tf_op jit(solution)/shard_map/ppermute | solution.py:513
  96.1 3.6 %collective-permute-start.16 = (bf16[768,768]{1,0:T(8,128)(2,1)}, bf16[768,768]{1,0:T(8,128)(2,1)S(1)}, u32[]{:S(2)}, u32[]{:S(2)}) collective-permute-start(bf16[768,768]{1,0:T(8,128)(2,1)} %together.8.refs_2_.refs_5_.refs_7_), channel_id=1, source_target_pairs={{0,1},{1,0},{2,3},{3,2},{4,5},{5,4},{6,7},{7,6},{8,9},{9,8},{10,11... | collective-permute-start | bytes 3538952 | tf_op jit(solution)/shard_map/ppermute | solution.py:513
  125.2 2.8 collective-permute-start.17
  128.4 14.7 %copy-start.10 = (bf16[768,768]{1,0:T(8,128)(2,1)}, bf16[768,768]{1,0:T(8,128)(2,1)S(1)}, u32[]{:S(2)}) copy-start(bf16[768,768]{1,0:T(8,128)(2,1)S(1)} %add_convert_fusion.1.refs_7_) | copy-start | bytes 3538948
  128.4 62.0 %collective-permute-start.18 = (bf16[768,768]{1,0:T(8,128)(2,1)S(1)}, bf16[768,768]{1,0:T(8,128)(2,1)S(1)}, u32[]{:S(2)}, u32[]{:S(2)}) collective-permute-start(bf16[768,768]{1,0:T(8,128)(2,1)S(1)} %add_convert_fusion.1.refs_7_), channel_id=1, source_target_pairs={{0,2},{1,3},{2,0},{3,1},{4,6},{5,7},{6,4},{7,5},{8,10},{9,11},{10,... | collective-permute-start | bytes 3538952 | tf_op jit(solution)/shard_map/ppermute | solution.py:513
  129.7 60.7 %collective-permute-start.24 = (bf16[192,768]{1,0:T(8,128)(2,1)S(1)}, bf16[192,768]{1,0:T(8,128)(2,1)S(1)}, u32[]{:S(2)}, u32[]{:S(2)}) collective-permute-start(bf16[192,768]{1,0:T(8,128)(2,1)S(1)} %copy-done.22), channel_id=1, source_target_pairs={{0,3},{1,2},{2,1},{3,0},{4,7},{5,6},{6,5},{7,4},{8,11},{9,10},{10,... | collective-permute-start | bytes 884744 | tf_op jit(solution)/shard_map/ppermute | solution.py:513
  130.6 59.7 %collective-permute-start.23 = (bf16[192,768]{1,0:T(8,128)(2,1)S(1)}, bf16[192,768]{1,0:T(8,128)(2,1)S(1)}, u32[]{:S(2)}, u32[]{:S(2)}) collective-permute-start(bf16[192,768]{1,0:T(8,128)(2,1)S(1)} %copy-done.22), channel_id=1, source_target_pairs={{0,2},{1,3},{2,0},{3,1},{4,6},{5,7},{6,4},{7,5},{8,10},{9,11},{10,... | collective-permute-start | bytes 884744 | tf_op jit(solution)/shard_map/ppermute | solution.py:513
  131.2 59.2 %collective-permute-start.22 = (bf16[192,768]{1,0:T(8,128)(2,1)S(1)}, bf16[192,768]{1,0:T(8,128)(2,1)S(1)}, u32[]{:S(2)}, u32[]{:S(2)}) collective-permute-start(bf16[192,768]{1,0:T(8,128)(2,1)S(1)} %copy-done.22), channel_id=1, source_target_pairs={{0,1},{1,0},{2,3},{3,2},{4,5},{5,4},{6,7},{7,6},{8,9},{9,8},{10,11... | collective-permute-start | bytes 884744 | tf_op jit(solution)/shard_map/ppermute | solution.py:513
  191.6 11.6 %copy-start.27 = (bf16[192,768]{1,0:T(8,128)(2,1)S(1)}, bf16[192,768]{1,0:T(8,128)(2,1)}, u32[]{:S(2)}) copy-start(bf16[192,768]{1,0:T(8,128)(2,1)} %get-tuple-element.69.refs_1_) | copy-start | bytes 884740
  191.6 13.1 %copy-start.26 = (bf16[192,768]{1,0:T(8,128)(2,1)S(1)}, bf16[192,768]{1,0:T(8,128)(2,1)}, u32[]{:S(2)}) copy-start(bf16[192,768]{1,0:T(8,128)(2,1)} %get-tuple-element.70.refs_2_) | copy-start | bytes 884740
  202.6 3.1 %collective-permute-start.25 = (bf16[768,768]{1,0:T(8,128)(2,1)}, bf16[768,768]{1,0:T(8,128)(2,1)S(1)}, u32[]{:S(2)}, u32[]{:S(2)}) collective-permute-start(bf16[768,768]{1,0:T(8,128)(2,1)} %get-tuple-element.78), channel_id=1, source_target_pairs={{0,1},{1,0},{2,3},{3,2},{4,5},{5,4},{6,7},{7,6},{8,9},{9,8},{10,11... | collective-permute-start | bytes 3538952 | tf_op jit(solution)/shard_map/ppermute | solution.py:513
  202.9 50.4 %collective-permute-start.10 = (bf16[768,768]{1,0:T(8,128)(2,1)}, bf16[768,768]{1,0:T(8,128)(2,1)}, u32[]{:S(2)}, u32[]{:S(2)}) collective-permute-start(bf16[768,768]{1,0:T(8,128)(2,1)} %get-tuple-element.57), channel_id=1, source_target_pairs={{0,1},{1,0},{2,3},{3,2},{4,5},{5,4},{6,7},{7,6},{8,9},{9,8},{10,11... | collective-permute-start | bytes 3538952 | tf_op jit(solution)/shard_map/ppermute | solution.py:513
  203.2 9.8 %collective-permute-start.20 = (bf16[192,768]{1,0:T(8,128)(2,1)S(1)}, bf16[192,768]{1,0:T(8,128)(2,1)S(1)}, u32[]{:S(2)}, u32[]{:S(2)}) collective-permute-start(bf16[192,768]{1,0:T(8,128)(2,1)S(1)} %copy-done.27), channel_id=1, source_target_pairs={{0,2},{1,3},{2,0},{3,1},{4,6},{5,7},{6,4},{7,5},{8,10},{9,11},{10,... | collective-permute-start | bytes 884744 | tf_op jit(solution)/shard_map/ppermute | solution.py:513
  204.7 13.7 %collective-permute-start.21 = (bf16[192,768]{1,0:T(8,128)(2,1)S(1)}, bf16[192,768]{1,0:T(8,128)(2,1)S(1)}, u32[]{:S(2)}, u32[]{:S(2)}) collective-permute-start(bf16[192,768]{1,0:T(8,128)(2,1)S(1)} %copy-done.26), channel_id=1, source_target_pairs={{0,3},{1,2},{2,1},{3,0},{4,7},{5,6},{6,5},{7,4},{8,11},{9,10},{10,... | collective-permute-start | bytes 884744 | tf_op jit(solution)/shard_map/ppermute | solution.py:513
  207.4 59.2 %collective-permute-start.27 = (bf16[768,768]{1,0:T(8,128)(2,1)S(1)}, bf16[768,768]{1,0:T(8,128)(2,1)S(1)}, u32[]{:S(2)}, u32[]{:S(2)}) collective-permute-start(bf16[768,768]{1,0:T(8,128)(2,1)S(1)} %add_convert_fusion.refs_14_), channel_id=1, source_target_pairs={{0,2},{1,3},{2,0},{3,1},{4,6},{5,7},{6,4},{7,5},{8,10},{9,11},{10,... | collective-permute-start | bytes 3538952 | tf_op jit(solution)/shard_map/ppermute | solution.py:513
  231.6 4.2 %collective-permute-start.28 = (f32[8,768]{1,0:T(8,128)}, f32[8,768]{1,0:T(8,128)S(1)}, u32[]{:S(2)}, u32[]{:S(2)}) collective-permute-start(f32[8,768]{1,0:T(8,128)} %get-tuple-element.83), channel_id=1, source_target_pairs={{0,4},{4,0},{8,12},{12,8},{16,20},{20,16},{24,28},{28,24},{1,5},{5... | collective-permute-start | bytes 73736 | tf_op jit(solution)/shard_map/ppermute | solution.py:513
  235.8 14.6 %copy-start.31 = (f32[8,768]{1,0:T(8,128)}, f32[8,768]{1,0:T(8,128)S(1)}, u32[]{:S(2)}) copy-start(f32[8,768]{1,0:T(8,128)S(1)} %collective-permute-done.28.refs_1_) | copy-start | bytes 73732
  236.5 9.5 %collective-permute-start.32 = (f32[8,768]{1,0:T(8,128)S(1)}, f32[8,768]{1,0:T(8,128)S(1)}, u32[]{:S(2)}, u32[]{:S(2)}) collective-permute-start(f32[8,768]{1,0:T(8,128)S(1)} %add.72), channel_id=1, source_target_pairs={{0,24},{4,28},{8,16},{12,20},{16,8},{20,12},{24,0},{28,4},{1,25},{... | collective-permute-start | bytes 73736 | tf_op jit(solution)/shard_map/ppermute | solution.py:513
  241.8 12.3 %collective-permute-start.19 = (bf16[192,768]{1,0:T(8,128)(2,1)}, bf16[192,768]{1,0:T(8,128)(2,1)S(1)}, u32[]{:S(2)}, u32[]{:S(2)}) collective-permute-start(bf16[192,768]{1,0:T(8,128)(2,1)} %get-tuple-element.68.refs_2_), channel_id=1, source_target_pairs={{0,1},{1,0},{2,3},{3,2},{4,5},{5,4},{6,7},{7,6},{8,9},{9,8},{10,11... | collective-permute-start | bytes 884744 | tf_op jit(solution)/shard_map/ppermute | solution.py:513
  241.8 8.6 %collective-permute-start.31 = (f32[8,768]{1,0:T(8,128)S(1)}, f32[8,768]{1,0:T(8,128)S(1)}, u32[]{:S(2)}, u32[]{:S(2)}) collective-permute-start(f32[8,768]{1,0:T(8,128)S(1)} %add.72), channel_id=1, source_target_pairs={{0,16},{4,20},{8,24},{12,28},{16,0},{20,4},{24,8},{28,12},{1,17},{... | collective-permute-start | bytes 73736 | tf_op jit(solution)/shard_map/ppermute | solution.py:513
  246.0 4.5 %collective-permute-start.30 = (f32[8,768]{1,0:T(8,128)S(1)}, f32[8,768]{1,0:T(8,128)S(1)}, u32[]{:S(2)}, u32[]{:S(2)}) collective-permute-start(f32[8,768]{1,0:T(8,128)S(1)} %add.72), channel_id=1, source_target_pairs={{0,8},{4,12},{8,0},{12,4},{16,24},{20,28},{24,16},{28,20},{1,9},{5... | collective-permute-start | bytes 73736 | tf_op jit(solution)/shard_map/ppermute | solution.py:513
  250.4 25.5 %collective-permute-start.26 = (bf16[768,768]{1,0:T(8,128)(2,1)}, bf16[768,768]{1,0:T(8,128)(2,1)}, u32[]{:S(2)}, u32[]{:S(2)}) collective-permute-start(bf16[768,768]{1,0:T(8,128)(2,1)} %get-tuple-element.81), channel_id=1, source_target_pairs={{0,1},{1,0},{2,3},{3,2},{4,5},{5,4},{6,7},{7,6},{8,9},{9,8},{10,11... | collective-permute-start | bytes 3538952 | tf_op jit(solution)/shard_map/ppermute | solution.py:513
  250.5 16.1 %collective-permute-start.29 = (bf16[2,2,96,768]{3,2,1,0:T(8,128)(2,1)}, bf16[2,2,96,768]{3,2,1,0:T(8,128)(2,1)S(1)}, u32[]{:S(2)}, u32[]{:S(2)}) collective-permute-start(bf16[2,2,96,768]{3,2,1,0:T(8,128)(2,1)} %together.9), channel_id=1, source_target_pairs={{0,4},{4,0},{8,12},{12,8},{16,20},{20,16},{24,28},{28,24},{1,5},{5... | collective-permute-start | bytes 1769480 | tf_op jit(solution)/shard_map/ppermute | solution.py:513
  253.3 7.9 %collective-permute-start.35 = (f32[8,768]{1,0:T(8,128)S(1)}, f32[8,768]{1,0:T(8,128)S(1)}, u32[]{:S(2)}, u32[]{:S(2)}) collective-permute-start(f32[8,768]{1,0:T(8,128)S(1)} %add_add_fusion.1), channel_id=1, source_target_pairs={{0,3},{1,2},{2,1},{3,0},{4,7},{5,6},{6,5},{7,4},{8,11},{9,10},{10,... | collective-permute-start | bytes 73736 | tf_op jit(solution)/shard_map/ppermute | solution.py:513
  260.0 3.9 %collective-permute-start.34 = (f32[8,768]{1,0:T(8,128)S(1)}, f32[8,768]{1,0:T(8,128)S(1)}, u32[]{:S(2)}, u32[]{:S(2)}) collective-permute-start(f32[8,768]{1,0:T(8,128)S(1)} %add_add_fusion.1), channel_id=1, source_target_pairs={{0,2},{1,3},{2,0},{3,1},{4,6},{5,7},{6,4},{7,5},{8,10},{9,11},{10,... | collective-permute-start | bytes 73736 | tf_op jit(solution)/shard_map/ppermute | solution.py:513
  261.2 2.8 collective-permute-start.33
  270.0 12.7 %collective-permute-start.38 = (bf16[96,768]{1,0:T(8,128)(2,1)S(1)}, bf16[96,768]{1,0:T(8,128)(2,1)S(1)}, u32[]{:S(2)}, u32[]{:S(2)}) collective-permute-start(bf16[96,768]{1,0:T(8,128)(2,1)S(1)} %get-tuple-element.132.refs_8_), channel_id=1, source_target_pairs={{0,24},{4,28},{8,16},{12,20},{16,8},{20,12},{24,0},{28,4},{1,25},{... | collective-permute-start | bytes 442376 | tf_op jit(solution)/shard_map/ppermute | solution.py:513
  272.9 13.3 %collective-permute-start.37 = (bf16[96,768]{1,0:T(8,128)(2,1)S(1)}, bf16[96,768]{1,0:T(8,128)(2,1)S(1)}, u32[]{:S(2)}, u32[]{:S(2)}) collective-permute-start(bf16[96,768]{1,0:T(8,128)(2,1)S(1)} %get-tuple-element.133.refs_7_), channel_id=1, source_target_pairs={{0,16},{4,20},{8,24},{12,28},{16,0},{20,4},{24,8},{28,12},{1,17},{... | collective-permute-start | bytes 442376 | tf_op jit(solution)/shard_map/ppermute | solution.py:513
  272.9 9.1 %collective-permute-start.36 = (bf16[96,768]{1,0:T(8,128)(2,1)S(1)}, bf16[96,768]{1,0:T(8,128)(2,1)S(1)}, u32[]{:S(2)}, u32[]{:S(2)}) collective-permute-start(bf16[96,768]{1,0:T(8,128)(2,1)S(1)} %get-tuple-element.134.refs_6_), channel_id=1, source_target_pairs={{0,8},{4,12},{8,0},{12,4},{16,24},{20,28},{24,16},{28,20},{1,9},{5... | collective-permute-start | bytes 442376 | tf_op jit(solution)/shard_map/ppermute | solution.py:513
  (35 other events, 95.1 us)
Sparse Core Ops, SparseCore 0:
  124.1 71.1 reduce-scatter.1
where the time goes:
time: 296 us; the launch traced here: 295 us
  Pallas kernels  152 us (51%)
  starting transfers between devices  49.7 us (17%)
  waiting for transfers between devices  42.5 us (14%)
  local copies, waits for them, and re-layouts  22 us (7%)
  other arithmetic  14.9 us (5%)
  between operations  14.5 us (5%)
    ppermute x39, starting transfers between devices, swap(): return lax.ppermute(value, axis, [(i, i ^ bit) for i in range(size)])  49.6 us
    pallas_call x1, Pallas kernels, attention(): pl.pallas_call(waiting(attention_kernel, 2, 5, len(deps)), grid_spec=pltp...  47.3 us
    pallas_call x2, Pallas kernels, feed_forward(): pl.pallas_call(waiting(ffn_kernel, 0, 8 + len(sofar), len(deps)), grid=(2...  44.9 us
    ppermute x39, waiting for transfers between devices, swap(): return lax.ppermute(value, axis, [(i, i ^ bit) for i in range(size)])  42.5 us
    pallas_call x2, Pallas kernels, finish(): pl.pallas_call(waiting(partial(finish_kernel, last), 1, 11 + len(sofar),...  23.4 us
    unnamed x89, local copies, waits for them, and re-layouts  14.1 us
    pallas_call x1, Pallas kernels, project(): pl.pallas_call(waiting(project_kernel, 1, 9, len(deps)), grid_spec=pltpu....  11.5 us
    pallas_call x4, Pallas kernels, merge(): pl.pallas_call(waiting(merge_kernel, 1, len(parts), len(deps)), grid_spec...  11.3 us
  transfers between devices with their start and end apart: 40, of which 17 were waited for; matrix products, arithmetic and copies ran while one was open for 8% of the time, Pallas kernels for 44%

commit v1 on v0

--- a/solution.py
+++ b/solution.py
@@ -124,10 +124,11 @@
     pdf = jnp.exp(-0.5 * up_pre * up_pre) * ((2.0 * math.pi) ** -0.5)
     hidden = (up_pre * cdf).astype(BF16)
     d_up = (d_hidden * (cdf + up_pre * pdf)).astype(BF16)
-    put_list([mlp_a, mlp_b], dot_nt(hidden, w_down_t[...]).astype(BF16))
+    branch = dot_nt(hidden, w_down_t[...]).astype(BF16)
     d_normed[...] = dot_nt(d_up, w_up[...]).astype(BF16)
     weight_g[:, :hid] += dot_tn(n, d_up)
     weight_g[:, hid:] += dot_tn(g, hidden)
+    put_list([mlp_a, mlp_b], branch)
     if last:
 
         @pl.when(pl.program_id(0) == pl.num_programs(0) - 1)
@@ -277,18 +278,18 @@
         allowed = (key >= first_key) & (key <= last_key)
         window = pl.ds(start, span)
         contexts = []
-        for h in range(heads):
-            rows = slice(h * HEAD_DIM, (h + 1) * HEAD_DIM)
-            scores = dot_nn(k_rows[h, window, :], q_t[rows])
-            scores = jnp.where(allowed, scores, MASKED)
+        head_rows = [slice(h * HEAD_DIM, (h + 1) * HEAD_DIM) for h in range(heads)]
+        all_scores = [dot_nn(k_rows[h, window, :], q_t[rows]) for h, rows in enumerate(head_rows)]
+        all_d_prob = [dot_nn(v_rows[h, window, :], do_t[rows]) for h, rows in enumerate(head_rows)]
+        for h, rows in enumerate(head_rows):
+            scores = jnp.where(allowed, all_scores[h], MASKED)
             highest = jnp.max(scores, axis=0, keepdims=True)
             expo = jnp.exp(scores - highest)
             prob = expo * (1.0 / jnp.sum(expo, axis=0, keepdims=True))
             prob_low = prob.astype(BF16)
             context = dot_nn(v_t[rows, window], prob_low)
-            d_prob = dot_nn(v_rows[h, window, :], do_t[rows])
             delta = jnp.sum(do_t[rows].astype(F32) * context, axis=0, keepdims=True)
-            d_scores = (prob * (d_prob - delta)).astype(BF16)
+            d_scores = (prob * (all_d_prob[h] - delta)).astype(BF16)
             dq_h = dot_nn(k_t[rows, window], d_scores) * scale
             dq[rows] = rope_t(dq_h, cos_here, -sin_here).astype(BF16)
             contexts.append(context.astype(BF16))
@@ -470,7 +471,7 @@
     mixed[...] = total.astype(BF16)
 
 
-def mix(tok, mlps, ctxs, weights, deps=(), block=384):
+def mix(tok, mlps, ctxs, chip_got, last_ctx, weights, deps=(), block=384):
     shard, width = tok.shape
     own = width // 4
     row = pl.BlockSpec((block, width), lambda b: (b, 0))
@@ -478,7 +479,9 @@
         waiting(mix_kernel, 0, 12, len(deps)),
         grid=(shard // block,),
         in_specs=[row] * 4
-        + [pl.BlockSpec((own, block), lambda b: (0, b))] * 4
+        + [pl.BlockSpec((own, block), lambda b: (0, b))] * 2
+        + [pl.BlockSpec((own, block), lambda b: (shard // own, b))]
+        + [pl.BlockSpec((own, block), lambda b: (0, b))]
         + [pl.BlockSpec((own, width), lambda b: (0, 0))] * 4
         + [pl.BlockSpec(memory_space=pl.ANY)] * len(deps),
         out_specs=row,
@@ -486,7 +489,7 @@
         compiler_params=params(),
         cost_estimate=cost(5),
         name="mix",
-    )(tok, *mlps, *ctxs, *weights, *deps)
+    )(tok, *mlps, *ctxs, chip_got, last_ctx, *weights, *deps)
 
 
 def together(*values, deps=()):
@@ -685,6 +688,7 @@
     near_mlp_core = to_core(near_mlp[1])
 
     qkv, d_ctx = project(me, [near_n, far_n], grad, wat, cosine, sine)
+    far_mlp_core = after(far_mlp_core, qkv)
     mlp_both = (far_mlp[0].astype(F32) + far_mlp_core.astype(F32)).astype(BF16)
     mlp_chip = to_chip(mlp_both)
     out_w = [own_out]
@@ -694,16 +698,17 @@
         low_block, me, qkv, d_ctx, begin, cosine, sine, (mlp_both,)
     )
 
-    ctxs = [ctx[0], to_core(ctx[1]), to_chip(ctx[2]), to_both(ctx[3])]
+    ctxs = [ctx[0], to_core(ctx[1])]
     far_dn, far_dn_b, *sofar = finish(
         me, ctx[2:], dq, kv, tok[2:], grad[2:], far_n, far_dm, wat, 2, (), (mlp_chip, *out_w[1:])
     )
     theirs = to_core(far_dn_b)
     both = (far_dn.astype(F32) + theirs.astype(F32)).astype(BF16)
-    dn_chip = to_chip(both)
+    away = jnp.concatenate([both, ctx[2], ctx[3]], axis=0)
+    chip_got = to_chip(away)
     near_dn, near_dn_b, sums, attn_g = finish(
         me, ctx[:2], dq, kv, tok[:2], grad[:2], near_n, near_dm, wat, 0, sofar,
-        (both, ctxs[2], ctxs[3], ffn_wg),
+        (away, ffn_wg),
     )
     dn_core = to_core(near_dn_b)
     attn_sum = Scatter(attn_g, n_dp, dp_me)
@@ -711,17 +716,18 @@
         attn_sum.send(bit)
         attn_sum.take()
         sums = sum_over(sums, "dp", n_dp, [bit])
-    first = swap(sums, "dp", n_dp, bits[2])
-    attn_sum.send(bits[2], (first,))
-    sums = sum_over(sums + first, "dp", n_dp, bits[:2])
-    sums = sum_over(sums, "row", n_row, [2, 1])
-    mixed = mix(tokens, [near_mlp[0], near_mlp_core, mlp_chip], ctxs, out_w)
-    attn_sum.theirs = after(attn_sum.theirs, sums, dn_chip, mixed)
+    attn_sum.send(bits[2])
+    sums = sum_over(after(sums, attn_sum.away), "dp", n_dp, bits[:2])
+    attn_sum.theirs = after(attn_sum.theirs, sums)
     attn_sum.take()
     attn_sum.send_last()
-    input_grad = input_gradient(
-        tokens, cotangent, [near_dn, dn_core, dn_chip], gain, attn_sum.aways
-    )
+    sums = sum_over(after(sums, *attn_sum.aways), "dp", n_dp, bits[2:3])
+    sums = sum_over(sums, "row", n_row, [2, 1])
+    last_ctx = to_core(chip_got[shard + own :])
+    mixed = mix(
+        tokens, [near_mlp[0], near_mlp_core, mlp_chip], ctxs, chip_got, last_ctx, out_w, attn_sum.aways
+    )
+    input_grad = input_gradient(tokens, cotangent, [near_dn, dn_core, chip_got], gain, (mixed,))
     attn_sum.parts[0] = after(attn_sum.parts[0], input_grad)
     attn_sum.take_last()
 

time: 296 us -> 275 us (0.929)
  Pallas kernels: 152 us -> 139 us
  waiting for transfers between devices: 42.5 us -> 33.5 us
  other arithmetic: 14.9 us -> 18 us
    pallas_call x1, Pallas kernels: 47.3 us -> 37.7 us  [attention(): pl.pallas_call(waiting(attention_kernel, 2, 5, len(deps)), grid_spec=pltp...]
    ppermute x39 -> x38, waiting for transfers between devices: 42.5 us -> 33.4 us  [swap(): return lax.ppermute(value, axis, [(i, i ^ bit) for i in range(size)])]
    pallas_call x2, Pallas kernels: 44.9 us -> 41.7 us  [feed_forward(): pl.pallas_call(waiting(ffn_kernel, 0, 8 + len(sofar), len(deps)), grid=(2...]
    ppermute x39 -> x38, starting transfers between devices: 49.6 us -> 47.4 us  [swap(): return lax.ppermute(value, axis, [(i, i ^ bit) for i in range(size)])]
    unnamed x89 -> x73, local copies, waits for them, and re-layouts: 14.1 us -> 13.1 us
  transfers between devices with their start and end apart: 40 -> 39, of which waited for: 17 -> 16; matrix products, arithmetic and copies ran while one was open for 8% -> 9% of each run, Pallas kernels for 44% -> 43%
where the time goes in v1:
time: 275 us; the launch traced here: 273 us
  Pallas kernels  139 us (51%)
  starting transfers between devices  47.5 us (17%)
  waiting for transfers between devices  33.5 us (12%)
  local copies, waits for them, and re-layouts  20.9 us (8%)
  other arithmetic  18 us (7%)
  between operations  14.5 us (5%)
    ppermute x38, starting transfers between devices, swap(): return lax.ppermute(value, axis, [(i, i ^ bit) for i in range(size)])  47.4 us
    pallas_call x2, Pallas kernels, feed_forward(): pl.pallas_call(waiting(ffn_kernel, 0, 8 + len(sofar), len(deps)), grid=(2...  41.7 us
    pallas_call x1, Pallas kernels, attention(): pl.pallas_call(waiting(attention_kernel, 2, 5, len(deps)), grid_spec=pltp...  37.7 us
    ppermute x38, waiting for transfers between devices, swap(): return lax.ppermute(value, axis, [(i, i ^ bit) for i in range(size)])  33.4 us
    pallas_call x2, Pallas kernels, finish(): pl.pallas_call(waiting(partial(finish_kernel, last), 1, 11 + len(sofar),...  23.3 us
    unnamed x73, local copies, waits for them, and re-layouts  13.1 us
    pallas_call x1, Pallas kernels, project(): pl.pallas_call(waiting(project_kernel, 1, 9, len(deps)), grid_spec=pltpu....  11.5 us
    pallas_call x4, Pallas kernels, merge(): pl.pallas_call(waiting(merge_kernel, 1, len(parts), len(deps)), grid_spec...  11.4 us
  transfers between devices with their start and end apart: 39, of which 16 were waited for; matrix products, arithmetic and copies ran while one was open for 9% of the time, Pallas kernels for 43%

profile of v1, /device:TPU:0, one launch (start us, length us, event | category | flops | bytes accessed | tf_op | source)
XLA Modules:
  0.0 273.1 jit_solution(11773087334690718359)
XLA Ops:
  7.2 3.0 %collective-permute-start.7 = (bf16[768,768]{1,0:T(8,128)(2,1)}, bf16[768,768]{1,0:T(8,128)(2,1)S(1)}, u32[]{:S(2)}, u32[]{:S(2)}) collective-permute-start(bf16[768,768]{1,0:T(8,128)(2,1)} %refs_0_.5), channel_id=1, source_target_pairs={{0,2},{1,3},{2,0},{3,1},{4,6},{5,7},{6,4},{7,5},{8,10},{9,11},{10,... | collective-permute-start | bytes 3538952 | tf_op jit(solution)/shard_map/ppermute | solution.py:516
  10.2 1.5 collective-permute-start.3
  11.7 2.6 collective-permute-start.2
  14.9 1.8 collective-permute-done.3
  16.7 5.3 %collective-permute-done.2 = bf16[96,768]{1,0:T(8,128)(2,1)S(1)} collective-permute-done((bf16[96,768]{1,0:T(8,128)(2,1)}, bf16[96,768]{1,0:T(8,128)(2,1)S(1)}, u32[]{:S(2)}, u32[]{:S(2)}) %collective-permute-start.2) | collective-permute-done | bytes 147488 | tf_op jit(solution)/shard_map/ppermute | solution.py:516
  22.7 2.6 merge.4
  26.1 3.3 %collective-permute-start.5 = (bf16[1,2,96,768]{3,2,1,0:T(8,128)(2,1)}, bf16[1,2,96,768]{3,2,1,0:T(8,128)(2,1)S(1)}, u32[]{:S(2)}, u32[]{:S(2)}) collective-permute-start(bf16[1,2,96,768]{3,2,1,0:T(8,128)(2,1)} %get-tuple-element.51), channel_id=1, source_target_pairs={{0,16},{4,20},{8,24},{12,28},{16,0},{20,4},{24,8},{28,12},{1,17},{... | collective-permute-start | bytes 884744 | tf_op jit(solution)/shard_map/ppermute | solution.py:516
  32.4 4.1 %collective-permute-done.6.refs_5_ = bf16[96,768]{1,0:T(8,128)(2,1)S(1)} collective-permute-done((bf16[96,768]{1,0:T(8,128)(2,1)S(1)}, bf16[96,768]{1,0:T(8,128)(2,1)S(1)}, u32[]{:S(2)}, u32[]{:S(2)}) %collective-permute-start.6) | collective-permute-done | bytes 147488 | tf_op jit(solution)/shard_map/ppermute | solution.py:516
  36.5 3.4 %collective-permute-done.4 = bf16[1,2,96,768]{3,2,1,0:T(8,128)(2,1)S(1)} collective-permute-done((bf16[1,2,96,768]{3,2,1,0:T(8,128)(2,1)}, bf16[1,2,96,768]{3,2,1,0:T(8,128)(2,1)S(1)}, u32[]{:S(2)}, u32[]{:S(2)}) %collective-permute-start.4) | collective-permute-done | bytes 294944 | tf_op jit(solution)/shard_map/ppermute | solution.py:516
  39.9 2.9 %collective-permute-done.5 = bf16[1,2,96,768]{3,2,1,0:T(8,128)(2,1)S(1)} collective-permute-done((bf16[1,2,96,768]{3,2,1,0:T(8,128)(2,1)}, bf16[1,2,96,768]{3,2,1,0:T(8,128)(2,1)S(1)}, u32[]{:S(2)}, u32[]{:S(2)}) %collective-permute-start.5) | collective-permute-done | bytes 294944 | tf_op jit(solution)/shard_map/ppermute | solution.py:516
  44.0 3.1 %merge.5 = (bf16[2,2,96,768]{3,2,1,0:T(8,128)(2,1)}, bf16[1,2,192,768]{3,2,1,0:T(8,128)(2,1)}) custom-call(s32[2]{0:T(128)} %pad_add_fusion.1.refs_0_, bf16[2,96,768]{2,1,0:T(8,128)(2,1)} %bitcast.70, bf16[2,96,768]{2,1,0:T(8,128)(2,1)} %bitcast.72, bf16[1,192,768]{2,1,0:T(8,128)(2,1)} %bitcast.71, bf16[1,192,768]{2,1,0:T(8,128)(2,1)} %bitcast.73, ...), custom_call_target="tpu_custom_call" | custom-call | flops 192240000 | bytes 1 | tf_op jit(solution)/shard_map/merge/pallas_call | solution.py:562
  49.2 1.6 fusion.5.refs_1_
  51.6 1.7 merge.7
  53.3 2.0 collective-permute-start.13
  55.4 2.9 %collective-permute-done.8 = bf16[2,2,96,768]{3,2,1,0:T(8,128)(2,1)} collective-permute-done((bf16[2,2,96,768]{3,2,1,0:T(8,128)(2,1)}, bf16[2,2,96,768]{3,2,1,0:T(8,128)(2,1)}, u32[]{:S(2)}, u32[]{:S(2)}) %collective-permute-start.8) | collective-permute-done | bytes 589856 | tf_op jit(solution)/shard_map/ppermute | solution.py:516
  58.3 3.2 %collective-permute-start.12 = (bf16[192,768]{1,0:T(8,128)(2,1)}, bf16[192,768]{1,0:T(8,128)(2,1)}, u32[]{:S(2)}, u32[]{:S(2)}) collective-permute-start(bf16[192,768]{1,0:T(8,128)(2,1)} %bitcast.62), channel_id=1, source_target_pairs={{0,16},{4,20},{8,24},{12,28},{16,0},{20,4},{24,8},{28,12},{1,17},{... | collective-permute-start | bytes 884744 | tf_op jit(solution)/shard_map/ppermute | solution.py:516
  62.1 2.7 %collective-permute-start.11 = (bf16[192,768]{1,0:T(8,128)(2,1)}, bf16[192,768]{1,0:T(8,128)(2,1)}, u32[]{:S(2)}, u32[]{:S(2)}) collective-permute-start(bf16[192,768]{1,0:T(8,128)(2,1)} %bitcast.63), channel_id=1, source_target_pairs={{0,8},{4,12},{8,0},{12,4},{16,24},{20,28},{24,16},{28,20},{1,9},{5... | collective-permute-start | bytes 884744 | tf_op jit(solution)/shard_map/ppermute | solution.py:516
  66.5 1.3 broadcast_in_dim.15.refs_5_
  69.4 3.9 %merge.6 = (bf16[4,2,96,768]{3,2,1,0:T(8,128)(2,1)}, bf16[2,2,192,768]{3,2,1,0:T(8,128)(2,1)}) custom-call(s32[2]{0:T(128)} %pad_add_fusion.refs_0_, bf16[4,96,768]{2,1,0:T(8,128)(2,1)} %bitcast.66, bf16[4,96,768]{2,1,0:T(8,128)(2,1)} %bitcast.14.refs_2_, bf16[2,192,768]{2,1,0:T(8,128)(2,1)} %bitcast.67, bf16[2,192,768]{2,1,0:T(8,128)(2,1)} %bitcast.16.refs_4_), custom_call_target="tpu_custom_call" | custom-call | flops 192240000 | bytes 1 | tf_op jit(solution)/shard_map/merge/pallas_call | solution.py:562
  73.3 20.4 %feed_forward.2 = (bf16[1536,768]{1,0:T(8,128)(2,1)}, bf16[768,768]{1,0:T(8,128)(2,1)}, bf16[768,768]{1,0:T(8,128)(2,1)}, bf16[1536,768]{1,0:T(8,128)(2,1)}, f32[768,1536]{1,0:T(8,128)}) custom-call(bf16[768,768]{1,0:T(8,128)(2,1)} %refs_0_.5, bf16[768,768]{1,0:T(8,128)(2,1)} %collective-permute-done.refs_1_.refs_6_, bf16[768,768]{1,0:T(8,128)(2,1)} %refs_1_.1, ...), custom_call_target="tpu_custom_call" | custom-call | flops 768960000 | bytes 1 | tf_op jit(solution)/shard_map/feed_forward/pallas_call | solution.py:152
  95.4 2.8 %assemble.1 = (bf16[768,768]{1,0:T(8,128)(2,1)}, bf16[192,768]{1,0:T(8,128)(2,1)}) custom-call(s32[1]{0:T(128)} %bitcast.25.me, bf16[192,768]{1,0:T(8,128)(2,1)} %bitcast.65, bf16[192,768]{1,0:T(8,128)(2,1)} %collective-permute-done.11.refs_2_.part_b, bf16[192,768]{1,0:T(8,128)(2,1)} %collective-permute-done.12.refs_3_.part_c, ...), custom_call_target="tpu_custom_call" | custom-call | flops 288360000 | bytes 1 | tf_op jit(solution)/shard_map/assemble/pallas_call | solution.py:182
  99.6 21.2 %feed_forward.3 = (bf16[1536,768]{1,0:T(8,128)(2,1)}, bf16[768,768]{1,0:T(8,128)(2,1)}, bf16[768,768]{1,0:T(8,128)(2,1)}, bf16[1536,768]{1,0:T(8,128)(2,1)}, bf16[768,1536]{1,0:T(8,128)(2,1)}) custom-call(bf16[768,768]{1,0:T(8,128)(2,1)} %copy-done, bf16[768,768]{1,0:T(8,128)(2,1)} %copy-done.8, bf16[768,768]{1,0:T(8,128)(2,1)} %together.10.refs_2_.refs_5_.refs_7_, ...), custom_call_target="tpu_custom_call" | custom-call | flops 768960000 | bytes 1 | tf_op jit(solution)/shard_map/feed_forward/pallas_call | solution.py:152
  121.1 11.5 %project.1 = (bf16[576,3072]{1,0:T(8,128)(2,1)}, bf16[192,3072]{1,0:T(8,128)(2,1)}) custom-call(s32[1]{0:T(128)} %bitcast.26.refs_0_.refs_1_, bf16[1536,768]{1,0:T(8,128)(2,1)} %get-tuple-element.63.refs_1_.refs_9_, bf16[1536,768]{1,0:T(8,128)(2,1)} %get-tuple-element.64.refs_2_.refs_9_, bf16[768,768]{1,0:T(8,128)(2,1)} %refs_1_.1, ...), custom_call_target="tpu_custom_call" | custom-call | flops 1057320000 | bytes 1 | tf_op jit(solution)/shard_map/project/pallas_call | solution.py:223
  133.6 1.3 copy-done.15
  134.9 1.6 add_convert_fusion.1.refs_7_
  137.6 1.3 collective-permute-start.22
  139.5 37.7 %attention.1 = (bf16[192,768]{1,0:T(8,128)(2,1)}, bf16[192,768]{1,0:T(8,128)(2,1)}, bf16[192,768]{1,0:T(8,128)(2,1)}, bf16[192,768]{1,0:T(8,128)(2,1)}, bf16[192...) custom-call(s32[12]{0:T(128)} %and_select_fusion.refs_0_, s32[1]{0:T(128)} %bitcast.26.refs_0_.refs_1_, ...), custom_call_target="tpu_custom_call" | custom-call | flops 4421519872 | bytes 1 | tf_op jit(solution)/shard_map/attention/pallas_call | solution.py:333
  178.7 10.9 %finish.2 = (bf16[768,768]{1,0:T(8,128)(2,1)}, bf16[768,768]{1,0:T(8,128)(2,1)}, f32[8,768]{1,0:T(8,128)}, f32[768,768]{1,0:T(8,128)}) custom-call(s32[1]{0:T(128)} %bitcast.26.refs_0_.refs_1_, bf16[192,768]{1,0:T(8,128)(2,1)} %get-tuple-element.69.refs_1_, bf16[192,768]{1,0:T(8,128)(2,1)} %get-tuple-element.70.refs_2_, ...), custom_call_target="tpu_custom_call" | custom-call | flops 961200000 | bytes 1 | tf_op jit(solution)/shard_map/finish/pallas_call | solution.py:414
  190.0 2.8 %collective-permute-done.23 = bf16[768,768]{1,0:T(8,128)(2,1)S(1)} collective-permute-done((bf16[768,768]{1,0:T(8,128)(2,1)}, bf16[768,768]{1,0:T(8,128)(2,1)S(1)}, u32[]{:S(2)}, u32[]{:S(2)}) %collective-permute-start.23) | collective-permute-done | bytes 1179680 | tf_op jit(solution)/shard_map/ppermute | solution.py:516
  192.8 1.7 add_convert_fusion
  194.6 1.6 collective-permute-start.24
  196.2 12.4 %finish.3 = (bf16[768,768]{1,0:T(8,128)(2,1)}, bf16[768,768]{1,0:T(8,128)(2,1)}, f32[8,768]{1,0:T(8,128)}, f32[768,768]{1,0:T(8,128)}) custom-call(s32[1]{0:T(128)} %bitcast.26.refs_0_.refs_1_, bf16[192,768]{1,0:T(8,128)(2,1)} %get-tuple-element.67.refs_1_.refs_4_, bf16[192,768]{1,0:T(8,128)(2,1)} %get-tuple-element.68.refs_2_, ...), custom_call_target="tpu_custom_call" | custom-call | flops 961200000 | bytes 1 | tf_op jit(solution)/shard_map/finish/pallas_call | solution.py:414
  208.6 2.2 fusion.refs_1_
  210.7 2.0 collective-permute-start.26
  212.7 7.1 %collective-permute-start.29 = (f32[8,768]{1,0:T(8,128)}, f32[8,768]{1,0:T(8,128)}, u32[]{:S(2)}, u32[]{:S(2)}) collective-permute-start(f32[8,768]{1,0:T(8,128)} %together.12), channel_id=1, source_target_pairs={{0,24},{4,28},{8,16},{12,20},{16,8},{20,12},{24,0},{28,4},{1,25},{... | collective-permute-start | bytes 73736 | tf_op jit(solution)/shard_map/ppermute | solution.py:516
  220.3 1.6 collective-permute-done.29.refs_2_
  221.9 2.9 %collective-permute-done.28.refs_1_ = f32[8,768]{1,0:T(8,128)} collective-permute-done((f32[8,768]{1,0:T(8,128)}, f32[8,768]{1,0:T(8,128)}, u32[]{:S(2)}, u32[]{:S(2)}) %collective-permute-start.28) | collective-permute-done | bytes 24608 | tf_op jit(solution)/shard_map/ppermute | solution.py:516
  224.8 1.4 add_add_fusion.1.refs_1_.refs_0_
  226.6 1.6 bitcast_add_fusion
  230.0 1.7 collective-permute-start.31
  231.7 2.3 collective-permute-done.31
  234.0 1.4 add.80
  235.4 1.5 collective-permute-start.19
  240.7 1.3 collective-permute-done.33.refs_1_
  242.1 7.1 %collective-permute-start.37 = (bf16[96,768]{1,0:T(8,128)(2,1)}, bf16[96,768]{1,0:T(8,128)(2,1)S(1)}, u32[]{:S(2)}, u32[]{:S(2)}) collective-permute-start(bf16[96,768]{1,0:T(8,128)(2,1)} %get-tuple-element.132.refs_14_.refs_3_), channel_id=1, source_target_pairs={{0,24},{4,28},{8,16},{12,20},{16,8},{20,12},{24,0},{28,4},{1,25},{... | collective-permute-start | bytes 442376 | tf_op jit(solution)/shard_map/ppermute | solution.py:516
  252.5 5.1 %mix.1.refs_6_ = bf16[768,768]{1,0:T(8,128)(2,1)} custom-call(bf16[768,768]{1,0:T(8,128)(2,1)} %refs_0_.5, bf16[768,768]{1,0:T(8,128)(2,1)} %get-tuple-element.56.refs_1_, bf16[768,768]{1,0:T(8,128)(2,1)} %collective-permute-done.10.refs_2_, bf16[768,768]{1,0:T(8,128)(2,1)} %copy-done.7, bf16[192,768]{1,0:T(8,128)(2,1)} %get-tuple-element.67.refs_1_.refs_4_, ...), custom_call_target="tpu_custom_call" | custom-call | flops 480600000 | bytes 1 | tf_op jit(solution)/shard_map/mix/pallas_call | solution.py:478
  257.7 5.3 %input_gradient.1.refs_1_ = bf16[768,768]{1,0:T(8,128)(2,1)} custom-call(bf16[768,768]{1,0:T(8,128)(2,1)} %refs_0_.5, bf16[768,768]{1,0:T(8,128)(2,1)} %refs_1_.1, bf16[768,768]{1,0:T(8,128)(2,1)} %get-tuple-element.85.refs_2_, bf16[768,768]{1,0:T(8,128)(2,1)} %collective-permute-done.30.refs_3_, bf16[1152,768]{1,0:T(8,128)(2,1)} %copy-done.5, ...), custom_call_target="tpu_custom_call" | custom-call | flops 480600000 | bytes 1 | tf_op jit(solution)/shard_map/input_gradient/pallas_call | solution.py:451
  263.6 1.1 fusion.1
  (157 shorter events, 33.0 us)
Async XLA Ops:
  7.2 189.0 %reduce-scatter.2.cloned.1.call-start = ((), (), s32[]{:S(2)}) async-start(), calls=%async_computation.1 | async-start | bytes 2654208 | tf_op jit(solution)/shard_map/reduce_scatter | solution.py:686
  7.2 35.6 %collective-permute-start.7 = (bf16[768,768]{1,0:T(8,128)(2,1)}, bf16[768,768]{1,0:T(8,128)(2,1)S(1)}, u32[]{:S(2)}, u32[]{:S(2)}) collective-permute-start(bf16[768,768]{1,0:T(8,128)(2,1)} %refs_0_.5), channel_id=1, source_target_pairs={{0,2},{1,3},{2,0},{3,1},{4,6},{5,7},{6,4},{7,5},{8,10},{9,11},{10,... | collective-permute-start | bytes 3538952 | tf_op jit(solution)/shard_map/ppermute | solution.py:516
  10.2 43.1 %collective-permute-start = (bf16[768,768]{1,0:T(8,128)(2,1)}, bf16[768,768]{1,0:T(8,128)(2,1)}, u32[]{:S(2)}, u32[]{:S(2)}) collective-permute-start(bf16[768,768]{1,0:T(8,128)(2,1)} %refs_0_.5), channel_id=1, source_target_pairs={{0,1},{1,0},{2,3},{3,2},{4,5},{5,4},{6,7},{7,6},{8,9},{9,8},{10,11... | collective-permute-start | bytes 3538952 | tf_op jit(solution)/shard_map/ppermute | solution.py:516
  10.2 6.5 %collective-permute-start.3 = (bf16[96,768]{1,0:T(8,128)(2,1)}, bf16[96,768]{1,0:T(8,128)(2,1)S(1)}, u32[]{:S(2)}, u32[]{:S(2)}) collective-permute-start(bf16[96,768]{1,0:T(8,128)(2,1)} %bitcast.79), channel_id=1, source_target_pairs={{0,4},{4,0},{8,12},{12,8},{16,20},{20,16},{24,28},{28,24},{1,5},{5... | collective-permute-start | bytes 442376 | tf_op jit(solution)/shard_map/ppermute | solution.py:516
  11.7 10.2 %collective-permute-start.2 = (bf16[96,768]{1,0:T(8,128)(2,1)}, bf16[96,768]{1,0:T(8,128)(2,1)S(1)}, u32[]{:S(2)}, u32[]{:S(2)}) collective-permute-start(bf16[96,768]{1,0:T(8,128)(2,1)} %param.18), channel_id=1, source_target_pairs={{0,16},{4,20},{8,24},{12,28},{16,0},{20,4},{24,8},{28,12},{1,17},{... | collective-permute-start | bytes 442376 | tf_op jit(solution)/shard_map/ppermute | solution.py:516
  25.3 14.6 %collective-permute-start.4 = (bf16[1,2,96,768]{3,2,1,0:T(8,128)(2,1)}, bf16[1,2,96,768]{3,2,1,0:T(8,128)(2,1)S(1)}, u32[]{:S(2)}, u32[]{:S(2)}) collective-permute-start(bf16[1,2,96,768]{3,2,1,0:T(8,128)(2,1)} %get-tuple-element.50), channel_id=1, source_target_pairs={{0,8},{4,12},{8,0},{12,4},{16,24},{20,28},{24,16},{28,20},{1,9},{5... | collective-permute-start | bytes 884744 | tf_op jit(solution)/shard_map/ppermute | solution.py:516
  26.1 16.8 %collective-permute-start.5 = (bf16[1,2,96,768]{3,2,1,0:T(8,128)(2,1)}, bf16[1,2,96,768]{3,2,1,0:T(8,128)(2,1)S(1)}, u32[]{:S(2)}, u32[]{:S(2)}) collective-permute-start(bf16[1,2,96,768]{3,2,1,0:T(8,128)(2,1)} %get-tuple-element.51), channel_id=1, source_target_pairs={{0,16},{4,20},{8,24},{12,28},{16,0},{20,4},{24,8},{28,12},{1,17},{... | collective-permute-start | bytes 884744 | tf_op jit(solution)/shard_map/ppermute | solution.py:516
  30.2 12.6 %copy-start.22 = (bf16[192,96]{0,1:T(8,128)(2,1)}, bf16[192,96]{0,1:T(8,128)(2,1)S(1)}, u32[]{:S(2)}) copy-start(bf16[192,96]{0,1:T(8,128)(2,1)S(1)} %copy.42) | copy-start | bytes 110596
  31.2 5.3 %collective-permute-start.6 = (bf16[96,768]{1,0:T(8,128)(2,1)S(1)}, bf16[96,768]{1,0:T(8,128)(2,1)S(1)}, u32[]{:S(2)}, u32[]{:S(2)}) collective-permute-start(bf16[96,768]{1,0:T(8,128)(2,1)S(1)} %pad_maximum_fusion.1), channel_id=1, source_target_pairs={{0,4},{4,0},{8,12},{12,8},{16,20},{20,16},{24,28},{28,24},{1,5},{5... | collective-permute-start | bytes 442376 | tf_op jit(solution)/shard_map/ppermute | solution.py:516
  36.5 6.3 %copy-start.28 = (bf16[96,768]{1,0:T(8,128)(2,1)}, bf16[96,768]{1,0:T(8,128)(2,1)S(1)}, u32[]{:S(2)}) copy-start(bf16[96,768]{1,0:T(8,128)(2,1)S(1)} %collective-permute-done.6.refs_5_) | copy-start | bytes 442372
  47.1 18.8 %copy-start.31 = (f32[768]{0:T(1024)S(1)}, f32[768]{0:T(1024)}, u32[]{:S(2)}) copy-start(f32[768]{0:T(1024)} %param.12) | copy-start | bytes 9220
  47.1 21.2 %copy-start.1 = (bf16[768,768]{1,0:T(8,128)(2,1)S(1)}, bf16[768,768]{1,0:T(8,128)(2,1)}, u32[]{:S(2)}) copy-start(bf16[768,768]{1,0:T(8,128)(2,1)} %copy-done) | copy-start | bytes 3538948
  47.1 11.2 %collective-permute-start.8 = (bf16[2,2,96,768]{3,2,1,0:T(8,128)(2,1)}, bf16[2,2,96,768]{3,2,1,0:T(8,128)(2,1)}, u32[]{:S(2)}, u32[]{:S(2)}) collective-permute-start(bf16[2,2,96,768]{3,2,1,0:T(8,128)(2,1)} %get-tuple-element.52), channel_id=1, source_target_pairs={{0,4},{4,0},{8,12},{12,8},{16,20},{20,16},{24,28},{28,24},{1,5},{5... | collective-permute-start | bytes 1769480 | tf_op jit(solution)/shard_map/ppermute | solution.py:516
  47.6 14.4 %collective-permute-start.9 = (bf16[1,2,192,768]{3,2,1,0:T(8,128)(2,1)}, bf16[1,2,192,768]{3,2,1,0:T(8,128)(2,1)}, u32[]{:S(2)}, u32[]{:S(2)}) collective-permute-start(bf16[1,2,192,768]{3,2,1,0:T(8,128)(2,1)} %get-tuple-element.53), channel_id=1, source_target_pairs={{0,8},{4,12},{8,0},{12,4},{16,24},{20,28},{24,16},{28,20},{1,9},{5... | collective-permute-start | bytes 1769480 | tf_op jit(solution)/shard_map/ppermute | solution.py:516
  48.0 45.9 %collective-permute-start.15 = (bf16[768,768]{1,0:T(8,128)(2,1)S(1)}, bf16[768,768]{1,0:T(8,128)(2,1)S(1)}, u32[]{:S(2)}, u32[]{:S(2)}) collective-permute-start(bf16[768,768]{1,0:T(8,128)(2,1)S(1)} %copy-done.2), channel_id=1, source_target_pairs={{0,2},{1,3},{2,0},{3,1},{4,6},{5,7},{6,4},{7,5},{8,10},{9,11},{10,... | collective-permute-start | bytes 3538952 | tf_op jit(solution)/shard_map/ppermute | solution.py:516
  48.5 24.8 %collective-permute-start.1 = (bf16[768,768]{1,0:T(8,128)(2,1)S(1)}, bf16[768,768]{1,0:T(8,128)(2,1)}, u32[]{:S(2)}, u32[]{:S(2)}) collective-permute-start(bf16[768,768]{1,0:T(8,128)(2,1)S(1)} %copy-done.2), channel_id=1, source_target_pairs={{0,1},{1,0},{2,3},{3,2},{4,5},{5,4},{6,7},{7,6},{8,9},{9,8},{10,11... | collective-permute-start | bytes 3538952 | tf_op jit(solution)/shard_map/ppermute | solution.py:516
  51.6 17.8 %copy-start.26 = (s32[3072]{0:T(1024)}, s32[3072]{0:T(1024)S(1)}, u32[]{:S(2)}) copy-start(s32[3072]{0:T(1024)S(1)} %select_reduce_fusion) | copy-start | bytes 36868
  53.3 40.4 %collective-permute-start.13 = (bf16[192,768]{1,0:T(8,128)(2,1)}, bf16[192,768]{1,0:T(8,128)(2,1)}, u32[]{:S(2)}, u32[]{:S(2)}) collective-permute-start(bf16[192,768]{1,0:T(8,128)(2,1)} %bitcast.61), channel_id=1, source_target_pairs={{0,24},{4,28},{8,16},{12,20},{16,8},{20,12},{24,0},{28,4},{1,25},{... | collective-permute-start | bytes 884744 | tf_op jit(solution)/shard_map/ppermute | solution.py:516
  58.3 35.4 %collective-permute-start.12 = (bf16[192,768]{1,0:T(8,128)(2,1)}, bf16[192,768]{1,0:T(8,128)(2,1)}, u32[]{:S(2)}, u32[]{:S(2)}) collective-permute-start(bf16[192,768]{1,0:T(8,128)(2,1)} %bitcast.62), channel_id=1, source_target_pairs={{0,16},{4,20},{8,24},{12,28},{16,0},{20,4},{24,8},{28,12},{1,17},{... | collective-permute-start | bytes 884744 | tf_op jit(solution)/shard_map/ppermute | solution.py:516
  62.1 31.7 %collective-permute-start.11 = (bf16[192,768]{1,0:T(8,128)(2,1)}, bf16[192,768]{1,0:T(8,128)(2,1)}, u32[]{:S(2)}, u32[]{:S(2)}) collective-permute-start(bf16[192,768]{1,0:T(8,128)(2,1)} %bitcast.63), channel_id=1, source_target_pairs={{0,8},{4,12},{8,0},{12,4},{16,24},{20,28},{24,16},{28,20},{1,9},{5... | collective-permute-start | bytes 884744 | tf_op jit(solution)/shard_map/ppermute | solution.py:516
  93.8 4.4 %collective-permute-start.14 = (bf16[768,768]{1,0:T(8,128)(2,1)}, bf16[768,768]{1,0:T(8,128)(2,1)S(1)}, u32[]{:S(2)}, u32[]{:S(2)}) collective-permute-start(bf16[768,768]{1,0:T(8,128)(2,1)} %together.9), channel_id=1, source_target_pairs={{0,1},{1,0},{2,3},{3,2},{4,5},{5,4},{6,7},{7,6},{8,9},{9,8},{10,11... | collective-permute-start | bytes 3538952 | tf_op jit(solution)/shard_map/ppermute | solution.py:516
  94.9 3.7 %collective-permute-start.16 = (bf16[768,768]{1,0:T(8,128)(2,1)}, bf16[768,768]{1,0:T(8,128)(2,1)S(1)}, u32[]{:S(2)}, u32[]{:S(2)}) collective-permute-start(bf16[768,768]{1,0:T(8,128)(2,1)} %together.10.refs_2_.refs_5_.refs_7_), channel_id=1, source_target_pairs={{0,1},{1,0},{2,3},{3,2},{4,5},{5,4},{6,7},{7,6},{8,9},{9,8},{10,11... | collective-permute-start | bytes 3538952 | tf_op jit(solution)/shard_map/ppermute | solution.py:516
  120.9 11.8 %collective-permute-start.17 = (bf16[768,768]{1,0:T(8,128)(2,1)}, bf16[768,768]{1,0:T(8,128)(2,1)S(1)}, u32[]{:S(2)}, u32[]{:S(2)}) collective-permute-start(bf16[768,768]{1,0:T(8,128)(2,1)} %get-tuple-element.62), channel_id=1, source_target_pairs={{0,1},{1,0},{2,3},{3,2},{4,5},{5,4},{6,7},{7,6},{8,9},{9,8},{10,11... | collective-permute-start | bytes 3538952 | tf_op jit(solution)/shard_map/ppermute | solution.py:516
  136.5 40.9 %collective-permute-start.18 = (bf16[768,768]{1,0:T(8,128)(2,1)S(1)}, bf16[768,768]{1,0:T(8,128)(2,1)S(1)}, u32[]{:S(2)}, u32[]{:S(2)}) collective-permute-start(bf16[768,768]{1,0:T(8,128)(2,1)S(1)} %add_convert_fusion.1.refs_7_), channel_id=1, source_target_pairs={{0,2},{1,3},{2,0},{3,1},{4,6},{5,7},{6,4},{7,5},{8,10},{9,11},{10,... | collective-permute-start | bytes 3538952 | tf_op jit(solution)/shard_map/ppermute | solution.py:516
  137.6 39.6 %collective-permute-start.22 = (bf16[192,768]{1,0:T(8,128)(2,1)}, bf16[192,768]{1,0:T(8,128)(2,1)S(1)}, u32[]{:S(2)}, u32[]{:S(2)}) collective-permute-start(bf16[192,768]{1,0:T(8,128)(2,1)} %get-tuple-element.74.refs_8_), channel_id=1, source_target_pairs={{0,3},{1,2},{2,1},{3,0},{4,7},{5,6},{6,5},{7,4},{8,11},{9,10},{10,... | collective-permute-start | bytes 884744 | tf_op jit(solution)/shard_map/ppermute | solution.py:516
  138.9 38.5 %collective-permute-start.21 = (bf16[192,768]{1,0:T(8,128)(2,1)}, bf16[192,768]{1,0:T(8,128)(2,1)S(1)}, u32[]{:S(2)}, u32[]{:S(2)}) collective-permute-start(bf16[192,768]{1,0:T(8,128)(2,1)} %get-tuple-element.74.refs_8_), channel_id=1, source_target_pairs={{0,2},{1,3},{2,0},{3,1},{4,6},{5,7},{6,4},{7,5},{8,10},{9,11},{10,... | collective-permute-start | bytes 884744 | tf_op jit(solution)/shard_map/ppermute | solution.py:516
  139.4 38.0 %collective-permute-start.20 = (bf16[192,768]{1,0:T(8,128)(2,1)}, bf16[192,768]{1,0:T(8,128)(2,1)S(1)}, u32[]{:S(2)}, u32[]{:S(2)}) collective-permute-start(bf16[192,768]{1,0:T(8,128)(2,1)} %get-tuple-element.74.refs_8_), channel_id=1, source_target_pairs={{0,1},{1,0},{2,3},{3,2},{4,5},{5,4},{6,7},{7,6},{8,9},{9,8},{10,11... | collective-permute-start | bytes 884744 | tf_op jit(solution)/shard_map/ppermute | solution.py:516
  189.7 3.1 %collective-permute-start.23 = (bf16[768,768]{1,0:T(8,128)(2,1)}, bf16[768,768]{1,0:T(8,128)(2,1)S(1)}, u32[]{:S(2)}, u32[]{:S(2)}) collective-permute-start(bf16[768,768]{1,0:T(8,128)(2,1)} %get-tuple-element.76), channel_id=1, source_target_pairs={{0,1},{1,0},{2,3},{3,2},{4,5},{5,4},{6,7},{7,6},{8,9},{9,8},{10,11... | collective-permute-start | bytes 3538952 | tf_op jit(solution)/shard_map/ppermute | solution.py:516
  194.6 43.3 %collective-permute-start.24 = (bf16[1152,768]{1,0:T(8,128)(2,1)S(1)}, bf16[1152,768]{1,0:T(8,128)(2,1)S(1)}, u32[]{:S(2)}, u32[]{:S(2)}) collective-permute-start(bf16[1152,768]{1,0:T(8,128)(2,1)S(1)} %pad_maximum_fusion.refs_14_), channel_id=1, source_target_pairs={{0,2},{1,3},{2,0},{3,1},{4,6},{5,7},{6,4},{7,5},{8,10},{9,11},{10,... | collective-permute-start | bytes 5308424 | tf_op jit(solution)/shard_map/ppermute | solution.py:516
  210.7 15.9 %collective-permute-start.26 = (bf16[2,2,96,768]{3,2,1,0:T(8,128)(2,1)}, bf16[2,2,96,768]{3,2,1,0:T(8,128)(2,1)}, u32[]{:S(2)}, u32[]{:S(2)}) collective-permute-start(bf16[2,2,96,768]{3,2,1,0:T(8,128)(2,1)} %fusion.refs_1_), channel_id=1, source_target_pairs={{0,4},{4,0},{8,12},{12,8},{16,20},{20,16},{24,28},{28,24},{1,5},{5... | collective-permute-start | bytes 1769480 | tf_op jit(solution)/shard_map/ppermute | solution.py:516
  212.7 9.2 %collective-permute-start.29 = (f32[8,768]{1,0:T(8,128)}, f32[8,768]{1,0:T(8,128)}, u32[]{:S(2)}, u32[]{:S(2)}) collective-permute-start(f32[8,768]{1,0:T(8,128)} %together.12), channel_id=1, source_target_pairs={{0,24},{4,28},{8,16},{12,20},{16,8},{20,12},{24,0},{28,4},{1,25},{... | collective-permute-start | bytes 73736 | tf_op jit(solution)/shard_map/ppermute | solution.py:516
  219.8 5.0 %collective-permute-start.28 = (f32[8,768]{1,0:T(8,128)}, f32[8,768]{1,0:T(8,128)}, u32[]{:S(2)}, u32[]{:S(2)}) collective-permute-start(f32[8,768]{1,0:T(8,128)} %together.12), channel_id=1, source_target_pairs={{0,16},{4,20},{8,24},{12,28},{16,0},{20,4},{24,8},{28,12},{1,17},{... | collective-permute-start | bytes 73736 | tf_op jit(solution)/shard_map/ppermute | solution.py:516
  219.8 5.0 %collective-permute-start.27 = (f32[8,768]{1,0:T(8,128)}, f32[8,768]{1,0:T(8,128)}, u32[]{:S(2)}, u32[]{:S(2)}) collective-permute-start(f32[8,768]{1,0:T(8,128)} %together.12), channel_id=1, source_target_pairs={{0,8},{4,12},{8,0},{12,4},{16,24},{20,28},{24,16},{28,20},{1,9},{5... | collective-permute-start | bytes 73736 | tf_op jit(solution)/shard_map/ppermute | solution.py:516
  221.9 28.6 %collective-permute-start.10 = (bf16[768,768]{1,0:T(8,128)(2,1)}, bf16[768,768]{1,0:T(8,128)(2,1)}, u32[]{:S(2)}, u32[]{:S(2)}) collective-permute-start(bf16[768,768]{1,0:T(8,128)(2,1)} %get-tuple-element.57), channel_id=1, source_target_pairs={{0,1},{1,0},{2,3},{3,2},{4,5},{5,4},{6,7},{7,6},{8,9},{9,8},{10,11... | collective-permute-start | bytes 3538952 | tf_op jit(solution)/shard_map/ppermute | solution.py:516
  224.8 32.8 %collective-permute-start.30 = (bf16[768,768]{1,0:T(8,128)(2,1)}, bf16[768,768]{1,0:T(8,128)(2,1)}, u32[]{:S(2)}, u32[]{:S(2)}) collective-permute-start(bf16[768,768]{1,0:T(8,128)(2,1)} %get-tuple-element.86), channel_id=1, source_target_pairs={{0,1},{1,0},{2,3},{3,2},{4,5},{5,4},{6,7},{7,6},{8,9},{9,8},{10,11... | collective-permute-start | bytes 3538952 | tf_op jit(solution)/shard_map/ppermute | solution.py:516
  230.0 4.0 %collective-permute-start.31 = (f32[8,768]{1,0:T(8,128)}, f32[8,768]{1,0:T(8,128)S(1)}, u32[]{:S(2)}, u32[]{:S(2)}) collective-permute-start(f32[8,768]{1,0:T(8,128)} %together.15), channel_id=1, source_target_pairs={{0,4},{4,0},{8,12},{12,8},{16,20},{20,16},{24,28},{28,24},{1,5},{5... | collective-permute-start | bytes 73736 | tf_op jit(solution)/shard_map/ppermute | solution.py:516
  235.4 3.8 %collective-permute-start.34 = (f32[8,768]{1,0:T(8,128)}, f32[8,768]{1,0:T(8,128)}, u32[]{:S(2)}, u32[]{:S(2)}) collective-permute-start(f32[8,768]{1,0:T(8,128)} %add.80), channel_id=1, source_target_pairs={{0,3},{1,2},{2,1},{3,0},{4,7},{5,6},{6,5},{7,4},{8,11},{9,10},{10,... | collective-permute-start | bytes 73736 | tf_op jit(solution)/shard_map/ppermute | solution.py:516
  235.4 15.2 %collective-permute-start.19 = (bf16[192,768]{1,0:T(8,128)(2,1)}, bf16[192,768]{1,0:T(8,128)(2,1)}, u32[]{:S(2)}, u32[]{:S(2)}) collective-permute-start(bf16[192,768]{1,0:T(8,128)(2,1)} %get-tuple-element.68.refs_2_), channel_id=1, source_target_pairs={{0,1},{1,0},{2,3},{3,2},{4,5},{5,4},{6,7},{7,6},{8,9},{9,8},{10,11... | collective-permute-start | bytes 884744 | tf_op jit(solution)/shard_map/ppermute | solution.py:516
  237.9 13.9 %copy-start.5 = (bf16[1152,768]{1,0:T(8,128)(2,1)}, bf16[1152,768]{1,0:T(8,128)(2,1)S(1)}, u32[]{:S(2)}) copy-start(bf16[1152,768]{1,0:T(8,128)(2,1)S(1)} %collective-permute-done.24.refs_6_.refs_4_) | copy-start | bytes 5308420
  237.9 12.6 %copy-start.12 = (bf16[96,768]{1,0:T(8,128)(2,1)S(1)}, bf16[96,768]{1,0:T(8,128)(2,1)}, u32[]{:S(2)}) copy-start(bf16[96,768]{1,0:T(8,128)(2,1)} %get-tuple-element.133.refs_13_.refs_2_) | copy-start | bytes 442372
  238.0 12.7 %copy-start.13 = (bf16[96,768]{1,0:T(8,128)(2,1)S(1)}, bf16[96,768]{1,0:T(8,128)(2,1)}, u32[]{:S(2)}) copy-start(bf16[96,768]{1,0:T(8,128)(2,1)} %get-tuple-element.134.refs_12_.refs_1_) | copy-start | bytes 442372
  238.0 4.1 %collective-permute-start.33 = (f32[8,768]{1,0:T(8,128)}, f32[8,768]{1,0:T(8,128)S(1)}, u32[]{:S(2)}, u32[]{:S(2)}) collective-permute-start(f32[8,768]{1,0:T(8,128)} %add.80), channel_id=1, source_target_pairs={{0,2},{1,3},{2,0},{3,1},{4,6},{5,7},{6,4},{7,5},{8,10},{9,11},{10,... | collective-permute-start | bytes 73736 | tf_op jit(solution)/shard_map/ppermute | solution.py:516
  239.2 10.0 %collective-permute-start.32 = (f32[8,768]{1,0:T(8,128)}, f32[8,768]{1,0:T(8,128)S(1)}, u32[]{:S(2)}, u32[]{:S(2)}) collective-permute-start(f32[8,768]{1,0:T(8,128)} %add.80), channel_id=1, source_target_pairs={{0,1},{1,0},{2,3},{3,2},{4,5},{5,4},{6,7},{7,6},{8,9},{9,8},{10,11... | collective-permute-start | bytes 73736 | tf_op jit(solution)/shard_map/ppermute | solution.py:516
  242.1 7.1 %copy-start.29 = (f32[8,768]{1,0:T(8,128)}, f32[8,768]{1,0:T(8,128)S(1)}, u32[]{:S(2)}) copy-start(f32[8,768]{1,0:T(8,128)S(1)} %collective-permute-done.33.refs_1_) | copy-start | bytes 73732
  242.1 21.5 %collective-permute-start.37 = (bf16[96,768]{1,0:T(8,128)(2,1)}, bf16[96,768]{1,0:T(8,128)(2,1)S(1)}, u32[]{:S(2)}, u32[]{:S(2)}) collective-permute-start(bf16[96,768]{1,0:T(8,128)(2,1)} %get-tuple-element.132.refs_14_.refs_3_), channel_id=1, source_target_pairs={{0,24},{4,28},{8,16},{12,20},{16,8},{20,12},{24,0},{28,4},{1,25},{... | collective-permute-start | bytes 442376 | tf_op jit(solution)/shard_map/ppermute | solution.py:516
  249.1 2.7 collective-permute-start.25
  250.6 13.1 %collective-permute-start.36 = (bf16[96,768]{1,0:T(8,128)(2,1)S(1)}, bf16[96,768]{1,0:T(8,128)(2,1)S(1)}, u32[]{:S(2)}, u32[]{:S(2)}) collective-permute-start(bf16[96,768]{1,0:T(8,128)(2,1)S(1)} %copy-done.12), channel_id=1, source_target_pairs={{0,16},{4,20},{8,24},{12,28},{16,0},{20,4},{24,8},{28,12},{1,17},{... | collective-permute-start | bytes 442376 | tf_op jit(solution)/shard_map/ppermute | solution.py:516
  250.7 12.3 %collective-permute-start.35 = (bf16[96,768]{1,0:T(8,128)(2,1)S(1)}, bf16[96,768]{1,0:T(8,128)(2,1)S(1)}, u32[]{:S(2)}, u32[]{:S(2)}) collective-permute-start(bf16[96,768]{1,0:T(8,128)(2,1)S(1)} %copy-done.13), channel_id=1, source_target_pairs={{0,8},{4,12},{8,0},{12,4},{16,24},{20,28},{24,16},{28,20},{1,9},{5... | collective-permute-start | bytes 442376 | tf_op jit(solution)/shard_map/ppermute | solution.py:516
  (26 other events, 45.7 us)
Sparse Core Ops, SparseCore 0:
  121.2 71.0 reduce-scatter.1
